TPU v7x, 128 devices: a whole 4x4x4 slice. The times are simulated.
128 devices in a mesh: pre: 8 (over y, core), dec: 16 (over x, z).
Axes of the slice: x: 4, y: 4, z: 4, core: 2. Of those that a mesh axis runs over, the one named last changes fastest.
Arguments:
- latent_cache: bfloat16 [64, 8192, 576], P(None, ('dec', 'pre')), may hold values from -29 to 29
- query: bfloat16 [64, 128, 576], P(None, 'dec'), may hold values from -4.5 to 4.5
- new_latent: bfloat16 [64, 576], replicated, may hold values from -9 to 9
- lengths: int32 [64], replicated, may hold values from 1 to 8192, 262144 in all
- slot_of: int32 [64], replicated, may hold values from 0 to 63, each once
- token_ids: int32 [64], replicated, may hold values from 0 to 129279
- latent_value_weight: bfloat16 [128, 512, 128], P('dec'), may hold values from -2 to 2
- out_weight: bfloat16 [16384, 7168], P('dec', 'pre'), may hold values from -0.046875 to 0.046875
- residual: bfloat16 [64, 7168], P(None, 'pre'), may hold values from -24 to 24
- norm_gain: bfloat16 [7168], P('pre'), may hold values from 0.5 to 1.5
- lm_weight: bfloat16 [7168, 129280], P('pre', 'dec'), may hold values from -6 to 6
Outputs:
- logprobs: float32 [64, 129280], P('pre', 'dec')
- target_logprob: float32 [64], P('pre')
Inputs may be any that keep to these rules, and one draw needn't show every extreme that they name: `slot_of`: each slot holds exactly one request.
All inputs are finite; a program needn't handle non-finite values.
Results may differ from a plain program's by a relative error of at most 0.0075.
Values may be sent and summed in bfloat16 or wider, within the bound.
A program may use at most 128 MiB of HBM per device.

v0:
```python
import jax
import jax.numpy as jnp
from jax import lax
from jax.sharding import PartitionSpec as P

KV_RANK = 512
ROPE = 64
VHEAD = 128
D = 7168


NEG_FILL = -1e30


def combined_all(value, axis, join):
    pieces = jax.tree.map(lambda part: lax.all_gather(part, axis), value)
    head = jax.tree.map(lambda part: part[0], pieces)
    tail = jax.tree.map(lambda part: part[1:], pieces)
    subtotal, _ = lax.scan(lambda subtotal, slab: (join(subtotal, slab), None), head, tail)
    return subtotal


def slot_holder(slots):
    amount = slots.shape[0]
    ordinal = jnp.arange(amount, dtype=jnp.int32)
    matches = slots[None, :] == ordinal[:, None]
    return jnp.sum(jnp.where(matches, ordinal[None, :], 0), axis=1)


def softmax_join(first, second):
    highest = jnp.maximum(first[0], second[0])
    scale_first = jnp.exp(first[0] - highest)
    scale_second = jnp.exp(second[0] - highest)
    totals = first[1] * scale_first + second[1] * scale_second
    accumulated = first[2] * scale_first[..., None] + second[2] * scale_second[..., None]
    return (highest, totals, accumulated)


def body(
    latent_cache,
    query,
    new_latent,
    lengths,
    slot_of,
    token_ids,
    latent_value_weight,
    out_weight,
    residual,
    norm_gain,
    lm_weight,
):
    dec_size = lax.axis_size("dec")
    pre_size = lax.axis_size("pre")
    requests = lengths.shape[0]
    per_device = requests // dec_size
    span_len = latent_cache.shape[1]
    lat_width = latent_cache.shape[2]
    heads_local = query.shape[1]
    heads_all = heads_local * dec_size
    given_holder = slot_holder(slot_of)
    used_holder = slot_holder(slot_of)
    cache_rows = jnp.take(latent_cache, used_holder, axis=0).reshape(requests, span_len * lat_width)
    query_rows = jnp.take(query, used_holder, axis=0).reshape(requests, heads_local * lat_width)
    cache_mine, query_mine = (
        lax.all_to_all(cache_rows, "dec", split_axis=0, concat_axis=1, tiled=True),
        lax.all_to_all(query_rows, "dec", split_axis=0, concat_axis=1, tiled=True),
    )
    local_len = dec_size * span_len
    cache_mine = cache_mine.reshape(per_device, local_len, lat_width)
    query_mine = query_mine.reshape(per_device, heads_all, lat_width)
    mine_requests = lax.dynamic_slice_in_dim(
        used_holder, lax.axis_index("dec") * per_device, per_device
    )
    mine_lengths = jnp.take(lengths, mine_requests)
    mine_new = jnp.take(new_latent, mine_requests, axis=0)
    prefill_index = lax.axis_index("pre")
    block_len = min(512, local_len // 2)
    blocks = local_len // block_len
    sm_scale = (VHEAD + ROPE) ** (-0.5)

    def position_of(local_index):
        return (
            local_index // span_len * pre_size + prefill_index
        ) * span_len + local_index % span_len

    def attend(operands):
        cache_one, query_one, length_one = operands

        def block_step(block_index, carried):
            block_start = block_index * block_len

            def live(current):
                running, totals, accumulated = current
                key_rows = lax.dynamic_slice_in_dim(cache_one, block_start, block_len, 0)
                key_spots = position_of(block_start + jnp.arange(block_len, dtype=jnp.int32))
                scores = (
                    lax.dot_general(
                        query_one,
                        key_rows,
                        (((1,), (1,)), ((), ())),
                        preferred_element_type=jnp.float32,
                    )
                    * sm_scale
                )
                scores = jnp.where(key_spots[None, :] < length_one, scores, NEG_FILL)
                highest = jnp.maximum(running, jnp.max(scores, axis=1))
                shrink = jnp.exp(running - highest)
                weights = jnp.exp(scores - highest[:, None])
                totals = totals * shrink + jnp.sum(weights, axis=1)
                accumulated = accumulated * shrink[:, None] + jnp.dot(
                    weights.astype(jnp.bfloat16),
                    key_rows[:, :KV_RANK],
                    preferred_element_type=jnp.float32,
                )
                return (highest, totals, accumulated)

            def skipped(current):
                return current

            return lax.cond(position_of(block_start) < length_one, live, skipped, carried)

        start_state = (
            jnp.full((heads_all,), NEG_FILL, jnp.float32),
            jnp.zeros((heads_all,), jnp.float32),
            jnp.zeros((heads_all, KV_RANK), jnp.float32),
        )
        return lax.fori_loop(0, blocks, block_step, start_state)

    partials = lax.map(attend, (cache_mine, query_mine, mine_lengths))
    running, totals, accumulated = combined_all(partials, "pre", softmax_join)
    own_scores = (
        jnp.einsum("rhw,rw->rh", query_mine, mine_new, preferred_element_type=jnp.float32)
        * sm_scale
    )
    highest = jnp.maximum(running, own_scores)
    shrink = jnp.exp(running - highest)
    own_weight = jnp.exp(own_scores - highest)
    totals = totals * shrink + own_weight
    own_values = mine_new[:, :KV_RANK].astype(jnp.float32)
    accumulated = (
        accumulated * shrink[..., None]
        + own_weight.astype(jnp.bfloat16).astype(jnp.float32)[..., None] * own_values[:, None, :]
    )
    latent_output = (accumulated / totals[..., None]).astype(jnp.bfloat16)
    head_row_block = lax.all_to_all(
        latent_output.reshape(per_device, heads_all * KV_RANK),
        "dec",
        split_axis=1,
        concat_axis=0,
        tiled=True,
    )
    head_row_block = head_row_block.reshape(requests, heads_local, KV_RANK)
    per_head_values = jnp.einsum(
        "yfg,fgu->yfu", head_row_block, latent_value_weight, preferred_element_type=jnp.float32
    ).astype(jnp.bfloat16)
    attn_part = jnp.dot(
        per_head_values.reshape(requests, heads_local * VHEAD),
        out_weight,
        preferred_element_type=jnp.float32,
    )
    attention_result = lax.psum(attn_part, "dec")
    hidden = jnp.take(residual, given_holder, axis=0).astype(jnp.float32) + attention_result
    square_part = jnp.sum(hidden * hidden, axis=1)
    scaled = (hidden * norm_gain.astype(jnp.float32)[None, :]).astype(jnp.bfloat16)
    logit_part = jnp.dot(scaled, lm_weight, preferred_element_type=jnp.float32)
    logit_sum, squared_total = (
        lax.psum_scatter(logit_part, "pre", scatter_dimension=0, tiled=True),
        lax.psum_scatter(square_part, "pre", scatter_dimension=0, tiled=True),
    )
    logits = logit_sum * lax.rsqrt(squared_total / D + 1e-06)[:, None]
    rows_here = logits.shape[0]
    vocab_here = logits.shape[1]
    slot_tokens = jnp.take(token_ids, given_holder)
    row_tokens = lax.dynamic_slice_in_dim(slot_tokens, prefill_index * rows_here, rows_here)
    columns = lax.axis_index("dec") * vocab_here + jnp.arange(vocab_here, dtype=jnp.int32)
    picked = jnp.sum(jnp.where(columns[None, :] == row_tokens[:, None], logits, 0.0), axis=1)
    local_max = jnp.max(logits, axis=1)
    highest_all = lax.pmax(local_max, "dec")
    local_sum = jnp.sum(jnp.exp(logits - highest_all[:, None]), axis=1)
    total_exp, target_logit = lax.psum((local_sum, picked), "dec")
    log_normalizer = highest_all + jnp.log(total_exp)
    return (logits - log_normalizer[:, None], target_logit - log_normalizer)


def solution(mesh):
    return jax.shard_map(
        body,
        mesh=mesh,
        in_specs=(
            P(None, ("dec", "pre"), None),
            P(None, "dec", None),
            P(),
            P(),
            P(),
            P(),
            P("dec", None, None),
            P("dec", "pre"),
            P(None, "pre"),
            P("pre"),
            P("pre", "dec"),
        ),
        out_specs=(P("pre", "dec"), P("pre")),
        check_vma=False,
    )
```

profile of v0, /device:TPU:0, one launch (start us, length us, event | category | flops | bytes accessed | tf_op | source)
XLA Modules:
  0.0 477.1 jit_solution(3865685239398964821)
XLA Ops:
  8.2 1.8 gather_fusion.3
  11.6 8.0 %all-to-all-start.1 = ((bf16[16,4,4608]{2,1,0:T(4,128)(2,1)}), bf16[16,4,4608]{2,1,0:T(4,128)(2,1)S(1)}, u32[]{:S(2)}, u32[]{:S(2)}) async-start(bf16[16,4,4608]{2,1,0:T(4,128)(2,1)} %broadcast_select_fusion.1), calls=%async_computation.1 | async-start | bytes 1179648 | tf_op jit(solution)/shard_map/all_to_all | solution.py:66
  19.6 6.0 %gather_fusion.2 = bf16[64,64,576]{2,1,0:T(8,128)(2,1)} fusion(bf16[64,64,576]{2,1,0:T(8,128)(2,1)} %param.19, s32[1024]{0:T(1024)S(1)} %pad_clamp_fusion.1), kind=kCustom, calls=%fused_computation.2 | custom fusion | bytes 9437440 | tf_op jit(solution)/shard_map/jit(_take)/gather | solution.py:62
  25.6 9.8 %gather.31 = bf16[16,4,36864]{2,1,0:T(4,128)(2,1)} reshape(bf16[64,64,576]{2,1,0:T(8,128)(2,1)} %gather_fusion.2) | data formatting | bytes 9437184 | tf_op jit(solution)/shard_map/jit(_take)/gather | solution.py:62
  35.4 6.6 %broadcast_select_fusion = bf16[16,4,36864]{2,1,0:T(4,128)(2,1)} fusion(bf16[16,4,36864]{2,1,0:T(4,128)(2,1)} %gather.31, pred[16,4]{1,0:T(8,128)(4,1)S(1)} %compare_and_fusion), kind=kLoop, calls=%fused_computation.44 | loop fusion | flops 2359296 | bytes 9437248 | tf_op jit(solution)/shard_map/jit(_take)/select_n | solution.py:62
  42.0 7.4 %all-to-all-start = ((bf16[16,4,36864]{2,1,0:T(4,128)(2,1)}), bf16[16,4,36864]{2,1,0:T(4,128)(2,1)}, u32[]{:S(2)}, u32[]{:S(2)}) async-start(bf16[16,4,36864]{2,1,0:T(4,128)(2,1)} %broadcast_select_fusion), calls=%async_computation | async-start | bytes 9437184 | tf_op jit(solution)/shard_map/all_to_all | solution.py:65
  51.7 67.3 %all-to-all-done = bf16[16,4,36864]{2,1,0:T(4,128)(2,1)} async-done(((bf16[16,4,36864]{2,1,0:T(4,128)(2,1)}), bf16[16,4,36864]{2,1,0:T(4,128)(2,1)}, u32[]{:S(2)}, u32[]{:S(2)}) %all-to-all-start) | async-done | bytes 4718624 | tf_op jit(solution)/shard_map/all_to_all | solution.py:65
  119.0 7.1 %copy.29 = bf16[4,16,36864]{2,1,0:T(8,128)(2,1)} copy(bf16[4,16,36864]{2,0,1:T(4,128)(2,1)} %bitcast.11) | data formatting | bytes 9437184 | tf_op jit(solution)/shard_map/all_to_all | solution.py:65
  126.1 9.9 %reshape.122 = bf16[4,1024,576]{2,1,0:T(8,128)(2,1)} reshape(bf16[4,16,36864]{2,1,0:T(8,128)(2,1)} %copy.29) | data formatting | bytes 9437184 | tf_op jit(solution)/shard_map/reshape | solution.py:69
  136.1 37.8 %while.63 = (s32[]{:T(128)}, f32[4,128]{1,0:T(4,128)S(1)}, f32[4,128]{1,0:T(4,128)S(1)}, f32[4,128,512]{2,1,0:T(8,128)}, s32[4]{0:T(128)S(1)}, /*index=5*/bf16[4...) while((s32[]{:T(128)}, f32[4,128]{1,0:T(4,128)S(1)}, ...), condition=%wide.region_8.9_spmd, body=%wide.region_1.8_spmd.sunk | while | flops 143209248 | bytes 6091705 | solution.py:129
  139.8 3.7 while.65
  140.5 2.4 conditional.2
  148.1 6.1 %while.65 = (s32[]{:T(128)}, f32[128]{0:T(128)S(1)}, f32[128]{0:T(128)S(1)}, f32[128,512]{1,0:T(8,128)S(1)}, s32[]{:T(128)}, /*index=5*/s32[]{:T(128)}, bf16[102...) while((s32[]{:T(128)}, f32[128]{0:T(128)S(1)}, ...), condition=%wide.region_7.7_spmd, body=%wide.region_2.6_spmd.sunk | while | flops 143209248 | bytes 2647624 | solution.py:127
  148.7 2.4 conditional.2
  151.8 2.4 conditional.2
  158.7 6.1 %while.65 = (s32[]{:T(128)}, f32[128]{0:T(128)S(1)}, f32[128]{0:T(128)S(1)}, f32[128,512]{1,0:T(8,128)S(1)}, s32[]{:T(128)}, /*index=5*/s32[]{:T(128)}, bf16[102...) while((s32[]{:T(128)}, f32[128]{0:T(128)S(1)}, ...), condition=%wide.region_7.7_spmd, body=%wide.region_2.6_spmd.sunk | while | flops 143209248 | bytes 2647624 | solution.py:127
  159.3 2.4 conditional.2
  162.4 2.4 conditional.2
  169.3 3.8 while.65
  170.0 2.4 conditional.2
  176.1 12.1 %all-gather.3 = f32[8,4,128]{2,1,0:T(4,128)S(1)} all-gather(f32[1,4,128]{2,1,0:T(4,128)S(1)} %bitcast.77), channel_id=2, replica_groups=mesh['pre'=8,'dec'=16] {'pre'}, dimensions={0}, use_global_device_ids=true | all-gather | bytes 18432 | tf_op jit(solution)/shard_map/all_gather | solution.py:16
  188.2 11.4 %all-gather.4 = f32[8,4,128]{2,1,0:T(4,128)S(1)} all-gather(f32[1,4,128]{2,1,0:T(4,128)S(1)} %bitcast.76), channel_id=3, replica_groups=mesh['pre'=8,'dec'=16] {'pre'}, dimensions={0}, use_global_device_ids=true | all-gather | bytes 18432 | tf_op jit(solution)/shard_map/all_gather | solution.py:16
  199.6 24.3 %all-gather.7.cloned.1.call-done = f32[32,128,512]{2,1,0:T(8,128)} async-done(((f32[4,128,512]{2,1,0:T(8,128)}), f32[32,128,512]{2,1,0:T(8,128)}) %all-gather.7.cloned.1.call-update) | async-done | bytes 8388624 | tf_op jit(solution)/shard_map/all_gather | solution.py:16
  223.9 7.6 %slice.58 = f32[28,128,512]{2,1,0:T(8,128)} slice(f32[32,128,512]{2,1,0:T(8,128)} %all-gather.7.cloned.1.call-done), slice={[4:32], [0:128], [0:512]} | slice | bytes 14680064 | tf_op jit(solution)/shard_map/slice | solution.py:18
  231.4 11.0 %while.64 = (s32[]{:T(128)}, f32[4,128]{1,0:T(4,128)S(1)}, f32[4,128]{1,0:T(4,128)S(1)}, f32[4,128,512]{2,1,0:T(8,128)S(1)}, f32[7,4,128]{2,1,0:T(4,128)S(1)}, /...) while((s32[]{:T(128)}, f32[4,128]{1,0:T(4,128)S(1)}, f32[4,128]{1,0:T(4,128)S(1)}, ...), condition=%wide.region_10.11_spmd, body=%wide.region_9.10_spmd.sunk | while | flops 789506 | bytes 3166309 | solution.py:19
  243.5 18.7 %all_to_all.42 = bf16[4,16,4096]{2,0,1:T(4,128)(2,1)S(1)} all-to-all(bf16[4,16,4096]{2,0,1:T(4,128)(2,1)S(1)} %copy.31), channel_id=1, replica_groups=mesh['pre'=8,'dec'=16] {'dec'}, dimensions={1} | all-to-all | bytes 1048576 | tf_op jit(solution)/shard_map/all_to_all | solution.py:145
  266.9 79.5 %all-reduce.4.cloned.1.call-done = f32[64,896]{1,0:T(8,128)} async-done(((f32[64,896]{1,0:T(8,128)}), f32[64,896]{1,0:T(8,128)}) %all-reduce.4.cloned.1.call-update) | async-done | bytes 229392 | tf_op jit(solution)/shard_map/psum | solution.py:161
  346.4 11.1 %fusion.24 = f32[64,8080]{1,0:T(8,128)} fusion(bf16[896,8080]{0,1:T(8,128)(2,1)} %param.29, f32[64,896]{1,0:T(8,128)} %all-reduce.4.cloned.1.call-done, f32[896]{0:T(1024)S(1)} %convert_element_type.45, bf16[64,896]{1,0:T(8,128)(2,1)S(1)} %gather_fusion, pred[64]{0:T(512)(128)(4,1)S(1)} %get-tuple-element.488), kind=kOutput, calls=%fused_computation.60 | convolution fusion | flops 926965760 | bytes 16895552 | tf_op jit(solution)/shard_map/dot_general | solution.py:165
  359.0 12.7 %all-reduce = f32[64]{0:T(128)S(1)} all-reduce(f32[64]{0:T(128)S(1)} %multiply_reduce_fusion), channel_id=6, replica_groups=mesh['pre'=8,'dec'=16] {'pre'}, use_global_device_ids=true, to_apply=%region_14.15.clone | all-reduce | flops 64 | bytes 512
  371.7 18.1 %reduce-scatter.2.cloned.1.call-done = f32[8,8080]{1,0:T(8,128)} async-done(((f32[64,8080]{1,0:T(8,128)}), f32[8,8080]{1,0:T(8,128)}) %reduce-scatter.2.cloned.1.call-update) | async-done | bytes 258576 | tf_op jit(solution)/shard_map/reduce_scatter | solution.py:167
  391.1 40.5 %pmax.7 = f32[8]{0:T(128)S(1)} all-reduce(f32[8]{0:T(128)S(1)} %multiply_reduce_fusion.1), channel_id=1, replica_groups=mesh['pre'=8,'dec'=16] {'dec'}, use_global_device_ids=true, to_apply=%region_16.17 | all-reduce | flops 8 | bytes 64 | tf_op jit(solution)/shard_map/pmax | solution.py:178
  432.8 35.5 %all-reduce.1 = (f32[8]{0:T(128)S(1)}, f32[8]{0:T(128)S(1)}) all-reduce(f32[8]{0:T(128)S(1)} %get-tuple-element.430, f32[8]{0:T(128)S(1)} %get-tuple-element.429), channel_id=1, replica_groups=mesh['pre'=8,'dec'=16] {'dec'}, use_global_device_ids=true, to_apply=%region_18.19 | all-reduce | flops 16 | bytes 128 | tf_op jit(solution)/shard_map/psum | solution.py:180
  (164 shorter events, 61.3 us)
Async XLA Ops:
  7.2 257.0 %copy-start = (bf16[1024,896]{1,0:T(8,128)(2,1)S(1)}, bf16[1024,896]{1,0:T(8,128)(2,1)}, u32[]{:S(2)}) copy-start(bf16[1024,896]{1,0:T(8,128)(2,1)} %param.26) | copy-start | bytes 5505028
  11.6 30.4 %all-to-all-start.1 = ((bf16[16,4,4608]{2,1,0:T(4,128)(2,1)}), bf16[16,4,4608]{2,1,0:T(4,128)(2,1)S(1)}, u32[]{:S(2)}, u32[]{:S(2)}) async-start(bf16[16,4,4608]{2,1,0:T(4,128)(2,1)} %broadcast_select_fusion.1), calls=%async_computation.1 | async-start | bytes 1179648 | tf_op jit(solution)/shard_map/all_to_all | solution.py:66
  42.0 7.6 %copy-start.1 = (s32[64]{0:T(128)S(1)}, s32[64]{0:T(128)}, u32[]{:S(2)}) copy-start(s32[64]{0:T(128)} %param.22) | copy-start | bytes 772
  42.0 77.0 %all-to-all-start = ((bf16[16,4,36864]{2,1,0:T(4,128)(2,1)}), bf16[16,4,36864]{2,1,0:T(4,128)(2,1)}, u32[]{:S(2)}, u32[]{:S(2)}) async-start(bf16[16,4,36864]{2,1,0:T(4,128)(2,1)} %broadcast_select_fusion), calls=%async_computation | async-start | bytes 9437184 | tf_op jit(solution)/shard_map/all_to_all | solution.py:65
  49.4 174.4 %all-gather.7.cloned.1.call-start = ((), (), s32[]{:S(2)}) async-start(), calls=%async_computation.6 | async-start | bytes 9437184 | tf_op jit(solution)/shard_map/all_gather | solution.py:16
  136.1 37.9 %copy-start.5 = (bf16[64,576]{1,0:T(8,128)(2,1)S(1)}, bf16[64,576]{1,0:T(8,128)(2,1)}, u32[]{:S(2)}) copy-start(bf16[64,576]{1,0:T(8,128)(2,1)} %param.21) | copy-start | bytes 221188
  173.9 172.5 %all-reduce.4.cloned.1.call-start = ((), (), s32[]{:S(2)}) async-start(), calls=%async_computation.4 | async-start | bytes 458752 | tf_op jit(solution)/shard_map/psum | solution.py:161
  223.9 7.6 %slice-start = ((f32[32,128,512]{2,1,0:T(8,128)}), f32[4,128,512]{2,1,0:T(8,128)S(1)}, s32[]{:S(2)}) async-start(f32[32,128,512]{2,1,0:T(8,128)} %all-gather.7.cloned.1.call-done), calls=%async_computation.7 | async-start | bytes 2097152 | tf_op jit(solution)/shard_map/slice | solution.py:17
  242.5 22.9 %copy-start.2 = (s32[64]{0:T(128)S(1)}, s32[64]{0:T(128)}, u32[]{:S(2)}) copy-start(s32[64]{0:T(128)} %param.24) | copy-start | bytes 772
  242.8 23.4 %copy-start.6 = (bf16[896]{0:T(1024)(128)(2,1)S(1)}, bf16[896]{0:T(1024)(128)(2,1)}, u32[]{:S(2)}) copy-start(bf16[896]{0:T(1024)(128)(2,1)} %param.28) | copy-start | bytes 5380
  242.8 23.4 %copy-start.3 = (bf16[64,896]{1,0:T(8,128)(2,1)S(1)}, bf16[64,896]{1,0:T(8,128)(2,1)}, u32[]{:S(2)}) copy-start(bf16[64,896]{1,0:T(8,128)(2,1)} %param.27) | copy-start | bytes 344068
  265.3 124.5 %reduce-scatter.2.cloned.1.call-start = ((), (), s32[]{:S(2)}) async-start(), calls=%async_computation.5 | async-start | bytes 2359296 | tf_op jit(solution)/shard_map/reduce_scatter | solution.py:167
  346.4 11.1 %copy-start.7 = (u32[128]{0:T(128)S(1)}, u32[128]{0:T(128)}, u32[]{:S(2)}) copy-start(u32[128]{0:T(128)} %constant.297) | copy-start | bytes 1540
  346.4 12.3 %copy-start.4 = (f32[64,896]{1,0:T(8,128)S(1)}, f32[64,896]{1,0:T(8,128)}, u32[]{:S(2)}) copy-start(f32[64,896]{1,0:T(8,128)} %all-reduce.4.cloned.1.call-done) | copy-start | bytes 688132
Sparse Core Ops, SparseCore 0:
  174.0 49.7 all-gather.6
  265.5 80.8 all-reduce.3
  357.6 32.2 reduce-scatter.1
where the time goes:
time: 479 us; the launch traced here: 477 us
  waiting for transfers between devices  189 us (39%)
  blocking collectives  131 us (27%)
  local copies, waits for them, and re-layouts  66.6 us (14%)
  other arithmetic  29.6 us (6%)
  matrix products  24.7 us (5%)
  starting transfers between devices  15.5 us (3%)
  between operations  14.7 us (3%)
  loops' own time  6.01 us (1%)
    psum x1, waiting for transfers between devices, body(): attention_result = lax.psum(attn_part, 'dec')  79.5 us
    all_to_all x1, waiting for transfers between devices, body(): lax.all_to_all(cache_rows, 'dec', split_axis=0, concat_axis=1, tiled=True)  67.3 us
    pmax x1, blocking collectives, body(): highest_all = lax.pmax(local_max, 'dec')  40.5 us
    psum x1, blocking collectives, body(): total_exp, target_logit = lax.psum((local_sum, picked), 'dec')  35.5 us
    all_gather x1, waiting for transfers between devices, combined_all(): pieces = jax.tree.map(lambda part: lax.all_gather(part, axis), value)  24.3 us
    all_gather x2, blocking collectives, combined_all(): pieces = jax.tree.map(lambda part: lax.all_gather(part, axis), value)  23.5 us
    all_to_all x1, blocking collectives, body(): lax.all_to_all(latent_output.reshape(per_device, heads_all * KV_RANK), 'd...  18.7 us
    reduce_scatter x1, waiting for transfers between devices, body(): lax.psum_scatter(logit_part, 'pre', scatter_dimension=0, tiled=True)  18.1 us
  transfers between devices with their start and end apart: 5, of which 4 were waited for; matrix products, arithmetic and copies ran while one was open for 6% of the time, Pallas kernels for 0%

commit v1 on v0

v1 whole, which is shorter than its diff:
```python
import functools

import jax
import jax.numpy as jnp
from jax import lax
from jax.experimental import pallas as pl
from jax.experimental.pallas import tpu as pltpu
from jax.sharding import PartitionSpec as P

KV_RANK = 512
ROPE = 64
VHEAD = 128
D = 7168
WIDTH = KV_RANK + ROPE
MESH = pl.DeviceIdType.MESH
FILL = -(2.0**100)
SCALE = (VHEAD + ROPE) ** (-0.5)
EXTRA = 128
HALF = 4096
CHUNKS = 4

PAIRS = ("x", "y", "y", "z")


def drain(ref, sem):
    pltpu.make_async_copy(ref, ref, sem).wait()


def kernel(
    lens, cache, query, newl, slots, toks, resid, gain, vw, ow, lm,
    out, tgt,
    kbuf, qbuf, pout, pin, vwv, owv, lmv, qown, lat, hv, rss, rsr, hsl, hid,
    sqs, sqr, ls, lr, lb, sms, smr,
    s_k, r_k, s_q, r_q, s_p, r_p, l_w, s_h, r_h, s_r, r_r, s_a, r_a, s_s, r_s,
    s_c, r_c, s_y, r_y, s_m, r_m,
):
    p, d = lax.axis_index("pre"), lax.axis_index("dec")
    y, c = lax.div(p, 2), lax.rem(p, 2)
    x, z = lax.div(d, 4), lax.rem(d, 4)
    vocab = lm.shape[1]

    def at(xx, yy, zz, cc):
        return (2 * yy + cc, 4 * xx + zz)

    def turn(value, step):
        return lax.rem(value + step, 4)

    def send(src, dst, ssem, rsem, device):
        pltpu.make_async_remote_copy(
            src_ref=src, dst_ref=dst, send_sem=ssem, recv_sem=rsem,
            device_id=device, device_id_type=MESH,
        ).start()

    def signal(device):
        pl.semaphore_signal(barrier, inc=1, device_id=device, device_id_type=MESH)

    DEC = [(i, j) for i in range(4) for j in range(4) if (i, j) != (0, 0)]
    PRE = [(i, j) for i in range(4) for j in range(2) if (i, j) != (0, 0)]

    barrier = pltpu.get_barrier_semaphore()
    for i, j in DEC:
        signal(at(turn(x, i), y, turn(z, j), c))
    for i, j in PRE:
        signal(at(x, turn(y, i), z, lax.rem(c + j, 2)))
    for i in (1, 2, 3):
        signal(at(turn(x, i), y, z, 1 - c))
        signal(at(x, y, turn(z, i), 1 - c))
    for i, j in DEC:
        signal(at(y, turn(y, i), turn(z, j), c))
        signal(at(turn(x, i), turn(y, j), y, c))

    @pl.when(x != y)
    def _():
        signal(at(y, y, z, c))

    @pl.when(z != y)
    def _():
        signal(at(x, y, y, c))

    pl.semaphore_wait(
        barrier,
        15 + 7 + 6 + 30 + (x != y).astype(jnp.int32) + (z != y).astype(jnp.int32),
    )

    def group_of(axis, xx, yy, zz, cc):
        return 2 * {"x": xx, "y": yy, "z": zz}[axis] + cc

    def send_cache(k):
        axis = PAIRS[k]
        mine = group_of(axis, x, y, z, c)
        for i, j in PRE:
            xx = turn(x, i) if axis == "x" else x
            yy = turn(y, i) if axis == "y" else y
            zz = turn(z, i) if axis == "z" else z
            cc = lax.rem(c + j, 2)
            send(
                cache.at[pl.ds(8 * group_of(axis, xx, yy, zz, cc) + 2 * k, 2)],
                kbuf.at[k, :, pl.ds(64 * mine, 64), :],
                s_k.at[k], r_k.at[k], at(xx, yy, zz, cc),
            )
        pltpu.make_async_copy(
            cache.at[pl.ds(8 * mine + 2 * k, 2)],
            kbuf.at[k, :, pl.ds(64 * mine, 64), :],
            r_k.at[k],
        ).start()

    QROWS = {"x": (0, 16), "y": (16, 32), "z": (48, 16)}
    QSEM = {"x": 0, "y": 1, "z": 2}

    def send_query(axis):
        first, rows = QROWS[axis]
        sem = QSEM[axis]
        for i, j in DEC:
            xx, zz = turn(x, i), turn(z, j)
            send(
                query.at[pl.ds(64 * group_of(axis, xx, y, zz, c) + first, rows)],
                qbuf.at[d, pl.ds(first, rows), :],
                s_q.at[sem], r_q.at[sem], at(xx, y, zz, c),
            )
        pltpu.make_async_copy(
            query.at[pl.ds(64 * group_of(axis, x, y, z, c) + first, rows)],
            qbuf.at[d, pl.ds(first, rows), :],
            r_q.at[sem],
        ).start()

    send_cache(1)
    send_query("y")
    send_query("x")
    send_query("z")
    send_cache(0)
    send_cache(3)
    send_cache(2)
    loads = [
        pltpu.make_async_copy(query.at[pl.ds(64 * p, 64)], qown, l_w.at[0]),
        pltpu.make_async_copy(vw, vwv, l_w.at[1]),
        pltpu.make_async_copy(ow, owv, l_w.at[2]),
        pltpu.make_async_copy(lm, lmv, l_w.at[3]),
    ]
    for load in loads:
        load.start()

    loads[0].wait()
    row = lax.broadcasted_iota(jnp.int32, (64, 64), 0)
    col = lax.broadcasted_iota(jnp.int32, (64, 64), 1)
    pick = (col == 8 * p + (row >> 3)).astype(jnp.float32).astype(jnp.bfloat16)
    new_rows = jnp.dot(pick, newl[...], preferred_element_type=jnp.float32)
    own = jnp.sum(qown[...].astype(jnp.float32) * new_rows, axis=1, keepdims=True) * SCALE
    to_slot = (slots[...] == row).astype(jnp.float32).astype(jnp.bfloat16)
    resid_slot = jnp.dot(to_slot, resid[...], preferred_element_type=jnp.float32)
    ls[:, :, :, pl.ds(HALF - 128, 128)] = jnp.zeros((2, 4, 16, 128), jnp.bfloat16)

    spot = lax.broadcasted_iota(jnp.int32, (1, 512), 1)
    lane = lax.broadcasted_iota(jnp.int32, (128, EXTRA), 1)

    def position(axis):
        slot, core, inner = spot >> 7, (spot >> 6) & 1, spot & 63
        xx = slot if axis == "x" else x
        yy = slot if axis == "y" else y
        zz = slot if axis == "z" else z
        return 64 * ((4 * xx + zz) * 8 + 2 * yy + core) + inner

    def attend(k):
        axis = PAIRS[k]
        drain(kbuf.at[k], r_k.at[k])
        spots = position(axis)
        group = group_of(axis, x, y, z, c)
        both = qbuf[:, pl.ds(16 * k, 16), :].astype(jnp.float32).reshape(16, 2, 8, WIDTH)
        sums, extras = [], []
        for j in range(2):
            rows = both[:, j].reshape(128, WIDTH).astype(jnp.bfloat16)
            keys = kbuf[k, j]
            scores = lax.dot_general(
                rows, keys, (((1,), (1,)), ((), ())), preferred_element_type=jnp.float32
            ) * SCALE
            scores = jnp.where(spots < lens[8 * group + 2 * k + j], scores, FILL)
            top = jnp.max(scores, axis=1, keepdims=True)
            top = top.astype(jnp.bfloat16).astype(jnp.float32)
            weights = jnp.exp(scores - top)
            total = jnp.sum(weights, axis=1, keepdims=True)
            sums.append(
                jnp.dot(
                    weights.astype(jnp.bfloat16), keys[:, :KV_RANK],
                    preferred_element_type=jnp.float32,
                ).reshape(16, 8, KV_RANK)
            )
            high = total.astype(jnp.bfloat16).astype(jnp.float32)
            extra = jnp.where(lane == 0, top, jnp.where(lane == 1, high, total - high))
            extras.append(extra.reshape(16, 8, EXTRA))
        pout[k, :, :, pl.ds(0, KV_RANK)] = jnp.concatenate(sums, axis=1).astype(jnp.bfloat16)
        pout[k, :, :, pl.ds(KV_RANK, EXTRA)] = jnp.concatenate(extras, axis=1).astype(jnp.bfloat16)
        yy = {"x": x, "y": y, "z": z}[axis]
        place = {"x": 4 * y + z, "y": d, "z": 4 * x + y}[axis]
        for i, j in DEC:
            xx, zz = turn(x, i), turn(z, j)
            send(
                pout.at[k, 4 * xx + zz], pin.at[k, place],
                s_p.at[k], r_p.at[k], at(xx, yy, zz, c),
            )

        def keep():
            pltpu.make_async_copy(pout.at[k, d], pin.at[k, place], r_p.at[k]).start()

        if axis == "y":
            keep()
        else:
            pl.when(yy == y)(keep)

            @pl.when(yy != y)
            def _():
                send(
                    pout.at[k, d], pin.at[k, place],
                    s_p.at[k], r_p.at[k], at(x, yy, z, c),
                )

    drain(qbuf.at[:, pl.ds(16, 32), :], r_q.at[1])
    attend(1)
    drain(qbuf.at[:, pl.ds(0, 16), :], r_q.at[0])
    attend(0)
    drain(qbuf.at[:, pl.ds(48, 16), :], r_q.at[2])
    attend(3)
    attend(2)

    for k in (1, 0, 3, 2):
        drain(pin.at[k], r_p.at[k])
        extra = pin[k, :, :, pl.ds(KV_RANK, EXTRA)].astype(jnp.float32)
        tops = extra[:, :, 0:1]
        totals = extra[:, :, 1:2] + extra[:, :, 2:3]
        own_k = own[16 * k:16 * k + 16]
        top = jnp.maximum(jnp.max(tops, axis=0), own_k)
        shrink = jnp.exp(tops - top[None])
        own_weight = jnp.exp(own_k - top)
        total = jnp.sum(totals * shrink, axis=0) + own_weight
        summed = (
            own_weight.astype(jnp.bfloat16).astype(jnp.float32)
            * new_rows[16 * k:16 * k + 16, :KV_RANK]
        )
        for s in range(16):
            summed = summed + shrink[s] * pin[k, s, :, pl.ds(0, KV_RANK)].astype(jnp.float32)
        summed = summed / total
        for b in range(KV_RANK // 128):
            lat[b, pl.ds(16 * k, 16), :] = summed[:, 128 * b:128 * b + 128]

    loads[1].wait()
    values = []
    for f in range(8):
        rows = jnp.concatenate(
            [lat[b, pl.ds(f, 8, stride=8), :] for b in range(KV_RANK // 128)], axis=1
        ).astype(jnp.bfloat16)
        values.append(jnp.dot(rows, vwv[f], preferred_element_type=jnp.float32))
    packed = jnp.concatenate(
        [jnp.concatenate(values[:4], axis=1), jnp.concatenate(values[4:], axis=1)], axis=0
    )
    hv[p] = packed.astype(jnp.bfloat16)
    for n, (i, j) in enumerate(PRE):
        send(hv.at[p], hv.at[p], s_h.at[n], r_h.at[n], at(x, turn(y, i), z, lax.rem(c + j, 2)))
    loads[2].wait()
    for n in range(7):
        drain(hv.at[0], r_h.at[n])

    heads = hv[...].astype(jnp.float32).reshape(8, 2, 8, KV_RANK)
    part = resid_slot * jnp.where(d == 0, 1.0, 0.0)
    for half in range(2):
        rows = heads[:, half].reshape(64, KV_RANK).astype(jnp.bfloat16)
        rows = jnp.dot(to_slot, rows, preferred_element_type=jnp.float32).astype(jnp.bfloat16)
        part = part + jnp.dot(
            rows, owv[pl.ds(KV_RANK * half, KV_RANK), :], preferred_element_type=jnp.float32
        )
    for s in range(16):
        rss[s] = part[4 * s:4 * s + 4]
    for n, (i, j) in enumerate(DEC):
        xx, zz = turn(x, i), turn(z, j)
        send(rss.at[4 * xx + zz], rsr.at[n], s_r.at[0], r_r.at[0], at(xx, y, zz, c))
    drain(rsr, r_r.at[0])
    hidden4 = rss[d]
    for n in range(15):
        hidden4 = hidden4 + rsr[n]
    hsl[d] = hidden4
    for n, (i, j) in enumerate(DEC):
        send(hsl.at[d], hsl.at[d], s_a.at[n], r_a.at[n], at(turn(x, i), y, turn(z, j), c))
    for n in range(15):
        drain(hsl.at[0], r_a.at[n])
    for s in range(16):
        hid[pl.ds(4 * s, 4), :] = hsl[s]
    hidden = hid[...]
    squares = jnp.sum(hidden * hidden, axis=1, keepdims=True)
    sqs[...] = jnp.broadcast_to(squares, (64, 128)).reshape(8, 8, 128)
    for n, (i, j) in enumerate(PRE):
        yy, cc = turn(y, i), lax.rem(c + j, 2)
        send(sqs.at[2 * yy + cc], sqr.at[n], s_s.at[0], r_s.at[0], at(x, yy, z, cc))
    scaled = (hidden * gain[...].astype(jnp.float32)).astype(jnp.bfloat16)

    wide = HALF // CHUNKS

    def join_cores(i):
        lanes = pl.ds(wide * i, wide)
        drain(lr.at[:, :, lanes], r_c.at[i])
        ls[c, :, :, lanes] = (
            ls[c, :, :, lanes].astype(jnp.float32) + lr[:, :, lanes].astype(jnp.float32)
        ).astype(jnp.bfloat16)
        for step in (1, 2, 3):
            yy = turn(y, step)
            send(
                ls.at[c, yy, :, lanes], lb.at[step - 1, :, lanes],
                s_y.at[i], r_y.at[i], at(x, yy, z, c),
            )

    loads[3].wait()
    for i in range(CHUNKS):
        for half in range(2):
            start = HALF * half + wide * i
            count = min(wide, vocab - start)
            product = jnp.dot(
                scaled, lmv[:, pl.ds(start, count)], preferred_element_type=jnp.float32
            ).reshape(8, 8, count).astype(jnp.bfloat16)
            for q in range(8):
                ls[q % 2, q // 2, pl.ds(8 * half, 8), pl.ds(wide * i, count)] = product[q]
        lanes = pl.ds(wide * i, wide)
        send(
            ls.at[1 - c, :, :, lanes], lr.at[:, :, lanes],
            s_c.at[i], r_c.at[i], at(x, y, z, 1 - c),
        )
        if i > 0:
            join_cores(i - 1)
    join_cores(CHUNKS - 1)

    drain(sqr, r_s.at[0])
    norm = sqs[p]
    for n in range(7):
        norm = norm + sqr[n]
    norm = lax.rsqrt(norm[:, 0:1] / D + 1e-06)
    for i in range(CHUNKS):
        drain(lb.at[:, :, pl.ds(wide * i, wide)], r_y.at[i])
    logits = ls[c, y].astype(jnp.float32)
    for n in range(3):
        logits = logits + lb[n].astype(jnp.float32)
    low, high = logits[:8] * norm, logits[8:] * norm

    column = lax.broadcasted_iota(jnp.int32, (8, HALF), 1)
    high = jnp.where(column < vocab - HALF, high, FILL)
    slot_rows = lax.broadcasted_iota(jnp.int32, (8, 64), 0) + 8 * p
    token = jnp.sum(jnp.where(slots[...] == slot_rows, toks[...], 0), axis=1, keepdims=True)
    token = token - d * vocab
    picked = jnp.sum(jnp.where(column == token, low, 0.0), axis=1, keepdims=True) + jnp.sum(
        jnp.where((column + HALF == token) & (column < vocab - HALF), high, 0.0),
        axis=1, keepdims=True,
    )
    top = jnp.maximum(
        jnp.max(low, axis=1, keepdims=True), jnp.max(high, axis=1, keepdims=True)
    )
    total = jnp.sum(jnp.exp(low - top), axis=1, keepdims=True) + jnp.sum(
        jnp.exp(high - top), axis=1, keepdims=True
    )
    lane8 = lax.broadcasted_iota(jnp.int32, (8, 128), 1)
    mine = jnp.where(lane8 == 0, top, jnp.where(lane8 == 1, total, picked))
    sms[...] = mine
    for n, (i, j) in enumerate(DEC):
        send(sms, smr.at[n], s_m.at[0], r_m.at[0], at(turn(x, i), y, turn(z, j), c))
    drain(smr, r_m.at[0])
    others = smr[...]
    best = jnp.maximum(jnp.max(others[:, :, 0:1], axis=0), top)
    total = total * jnp.exp(top - best) + jnp.sum(
        others[:, :, 1:2] * jnp.exp(others[:, :, 0:1] - best[None]), axis=0
    )
    picked = picked + jnp.sum(others[:, :, 2:3], axis=0)
    normalizer = best + jnp.log(total)
    out[:, pl.ds(0, HALF)] = low - normalizer
    out[:, pl.ds(HALF, vocab - HALF)] = (high - normalizer)[:, : vocab - HALF]
    tgt[...] = jnp.broadcast_to(picked - normalizer, (8, 128))

    for k in range(4):
        drain(kbuf.at[k, :, pl.ds(0, 448), :], s_k.at[k])
        drain(pin.at[k, pl.ds(0, 15)], s_p.at[k])
        if PAIRS[k] != "y":

            @pl.when({"x": x, "z": z}[PAIRS[k]] != y)
            def _():
                drain(pin.at[k, 0], s_p.at[k])

    for axis in "xyz":
        first, rows = QROWS[axis]
        drain(qbuf.at[pl.ds(0, 15), pl.ds(first, rows), :], s_q.at[QSEM[axis]])
    for n in range(7):
        drain(hv.at[0], s_h.at[n])
    drain(rsr, s_r.at[0])
    for n in range(15):
        drain(hsl.at[0], s_a.at[n])
    drain(sqr, s_s.at[0])
    for i in range(CHUNKS):
        drain(lr.at[:, :, pl.ds(wide * i, wide)], s_c.at[i])
        drain(lb.at[:, :, pl.ds(wide * i, wide)], s_y.at[i])
    drain(smr, s_m.at[0])


def body(
    latent_cache, query, new_latent, lengths, slot_of, token_ids,
    latent_value_weight, out_weight, residual, norm_gain, lm_weight,
):
    columns, vocab = lm_weight.shape
    bf16, f32 = jnp.bfloat16, jnp.float32
    vmem = pl.BlockSpec(memory_space=pltpu.VMEM)
    anywhere = pl.BlockSpec(memory_space=pl.ANY)
    smem = pl.BlockSpec(memory_space=pltpu.SMEM)
    dma = pltpu.SemaphoreType.DMA
    logprobs, target = pl.pallas_call(
        kernel,
        out_shape=(
            jax.ShapeDtypeStruct((8, vocab), f32),
            jax.ShapeDtypeStruct((8, 128), f32),
        ),
        in_specs=[smem, anywhere, anywhere, vmem, vmem, vmem, vmem, vmem,
                  anywhere, anywhere, anywhere],
        out_specs=(vmem, vmem),
        scratch_shapes=[
            pltpu.VMEM((4, 2, 512, WIDTH), bf16),
            pltpu.VMEM((16, 64, WIDTH), bf16),
            pltpu.VMEM((4, 16, 16, KV_RANK + EXTRA), bf16),
            pltpu.VMEM((4, 16, 16, KV_RANK + EXTRA), bf16),
            pltpu.VMEM((8, KV_RANK, VHEAD), bf16),
            pltpu.VMEM((1024, columns), bf16),
            pltpu.VMEM((columns, vocab), bf16),
            pltpu.VMEM((64, WIDTH), bf16),
            pltpu.VMEM((KV_RANK // 128, 64, 128), f32),
            pltpu.VMEM((8, 16, 512), bf16),
            pltpu.VMEM((16, 4, columns), f32),
            pltpu.VMEM((15, 4, columns), f32),
            pltpu.VMEM((16, 4, columns), f32),
            pltpu.VMEM((64, columns), f32),
            pltpu.VMEM((8, 8, 128), f32),
            pltpu.VMEM((7, 8, 128), f32),
            pltpu.VMEM((2, 4, 16, HALF), bf16),
            pltpu.VMEM((4, 16, HALF), bf16),
            pltpu.VMEM((3, 16, HALF), bf16),
            pltpu.VMEM((8, 128), f32),
            pltpu.VMEM((15, 8, 128), f32),
            dma((4,)), dma((4,)), dma((3,)), dma((3,)), dma((4,)), dma((4,)), dma((4,)),
            dma((7,)), dma((7,)), dma((1,)), dma((1,)), dma((15,)), dma((15,)),
            dma((1,)), dma((1,)), dma((CHUNKS,)), dma((CHUNKS,)), dma((CHUNKS,)),
            dma((CHUNKS,)), dma((1,)), dma((1,)),
        ],
        name="decode_step",
        compiler_params=pltpu.CompilerParams(
            collective_id=0, has_side_effects=True, vmem_limit_bytes=56 << 20
        ),
    )(
        lengths,
        latent_cache,
        query.reshape(-1, WIDTH),
        new_latent,
        slot_of.reshape(1, -1),
        token_ids.reshape(1, -1),
        residual,
        norm_gain.reshape(1, -1),
        latent_value_weight,
        out_weight,
        lm_weight,
    )
    return logprobs, target[:, 0]


def solution(mesh):
    return jax.shard_map(
        body,
        mesh=mesh,
        in_specs=(
            P(None, ("dec", "pre"), None),
            P(None, "dec", None),
            P(),
            P(),
            P(),
            P(),
            P("dec", None, None),
            P("dec", "pre"),
            P(None, "pre"),
            P("pre"),
            P("pre", "dec"),
        ),
        out_specs=(P("pre", "dec"), P("pre")),
        check_vma=False,
    )
```

time: 479 us -> 125 us (0.26)
  waiting for transfers between devices: 189 us -> 0 us
  blocking collectives: 131 us -> 0 us
  Pallas kernels: 0 us -> 100 us
  local copies, waits for them, and re-layouts: 66.6 us -> 23.5 us
  other arithmetic: 29.6 us -> 0 us
  matrix products: 24.7 us -> 0 us
  starting transfers between devices: 15.5 us -> 0 us
  between operations: 14.7 us -> 0.64 us
  loops' own time: 6.01 us -> 0 us
    pallas_call x0 -> x1, Pallas kernels: none -> 100 us  [body(): pl.pallas_call(kernel, out_shape=(jax.ShapeDtypeStruct((8, vocab), f32),...]
    psum x1 -> x0, waiting for transfers between devices: 79.5 us -> none  [body(): attention_result = lax.psum(attn_part, 'dec')]
    all_to_all x2 -> x0, waiting for transfers between devices: 67.3 us -> none  [the longest x1 67.3 us: body(): lax.all_to_all(cache_rows, 'dec', split_axis=0, concat_axis=1, tiled=True)]
    pmax x1 -> x0, blocking collectives: 40.5 us -> none  [body(): highest_all = lax.pmax(local_max, 'dec')]
    psum x1 -> x0, blocking collectives: 35.5 us -> none  [body(): total_exp, target_logit = lax.psum((local_sum, picked), 'dec')]
    dot_general x16 -> x0, matrix products: 24.7 us -> none  [the longest x1 11.1 us: body(): logit_part = jnp.dot(scaled, lm_weight, preferred_element_type=jnp.float32)]
    all_gather x1 -> x0, waiting for transfers between devices: 24.3 us -> none  [combined_all(): pieces = jax.tree.map(lambda part: lax.all_gather(part, axis), value)]
    all_gather x2 -> x0, blocking collectives: 23.5 us -> none  [combined_all(): pieces = jax.tree.map(lambda part: lax.all_gather(part, axis), value)]
  transfers between devices with their start and end apart: 5 -> 0, of which waited for: 4 -> 0; matrix products, arithmetic and copies ran while one was open for 6% -> 0% of each run, Pallas kernels for 0% -> 0%
where the time goes in v1:
time: 125 us; the launch traced here: 124 us
  Pallas kernels  100 us (80%)
  local copies, waits for them, and re-layouts  23.5 us (19%)
    pallas_call x1, Pallas kernels, body(): pl.pallas_call(kernel, out_shape=(jax.ShapeDtypeStruct((8, vocab), f32),...  100 us
    unnamed x2, local copies, waits for them, and re-layouts  21 us

profile of v1, /device:TPU:0, one launch (start us, length us, event | category | flops | bytes accessed | tf_op | source)
XLA Modules:
  0.0 124.3 jit_solution(8236626893148994253)
XLA Ops:
  0.6 1.3 %reshape.19.gain = bf16[1,896]{1,0:T(2,128)(2,1)} reshape(bf16[896]{0:T(1024)(128)(2,1)} %param.20) | data formatting | bytes 3584 | tf_op jit(solution)/shard_map/reshape | solution.py:452
  1.9 19.3 %copy.14.lm = bf16[896,8080]{1,0:T(8,128)(2,1)} copy(bf16[896,8080]{0,1:T(8,128)(2,1)} %param.21) | data formatting | bytes 28958720 | tf_op args[10]
  21.2 100.1 %decode_step.1 = (f32[8,8080]{1,0:T(8,128)}, f32[8,128]{1,0:T(8,128)}) custom-call(s32[64]{0:T(128)} %lens.1, bf16[64,64,576]{2,1,0:T(8,128)(2,1)} %cache.1, bf16[512,576]{1,0:T(8,128)(2,1)} %bitcast.3, bf16[64,576]{1,0:T(8,128)(2,1)} %newl.1, s32[1,64]{1,0:T(1,128)} %bitcast.4, s32[1,64]{1,0:T(1,128)} %bitcast.5, bf16[64,896]{1,0:T(8,128)(2,1)} %resid.1, ...), custom_call_target="tpu_custom_call" | custom-call | tf_op jit(solution)/shard_map/decode_step/pallas_call | solution.py:404
  121.3 1.3 %slice_reduce_fusion = f32[8]{0:T(128)} fusion(f32[8,128]{1,0:T(8,128)} %get-tuple-element.5), kind=kLoop, calls=%fused_computation | loop fusion | bytes 64 | tf_op jit(solution)/shard_map/slice | solution.py:457
  122.6 1.7 %copy.16 = f32[8,8080]{1,0:T(8,128)} copy(f32[8,8080]{1,0:T(8,128)} %get-tuple-element.8) | data formatting | bytes 517120

commit v2 on v1

--- a/solution.py
+++ b/solution.py
@@ -20,6 +20,8 @@
 CHUNKS = 4
 
 PAIRS = ("x", "y", "y", "z")
+EARLY = ("x", "z", "x", "z")
+FIRST = ("z", "x", "z", "x")
 
 
 def drain(ref, sem):
@@ -29,15 +31,15 @@
 def kernel(
     lens, cache, query, newl, slots, toks, resid, gain, vw, ow, lm,
     out, tgt,
-    kbuf, qbuf, pout, pin, vwv, owv, lmv, qown, lat, hv, rss, rsr, hsl, hid,
+    kbuf, qbuf, pout, pjoin, pmid, pin, vwv, owv, lmv, qown, lat, hv, resw, rss, rsr, agb,
     sqs, sqr, ls, lr, lb, sms, smr,
-    s_k, r_k, s_q, r_q, s_p, r_p, l_w, s_h, r_h, s_r, r_r, s_a, r_a, s_s, r_s,
+    s_k, r_k, s_q, r_q, s_v, r_v, s_p, r_p, s_j, r_j, l_w, s_h, r_h, s_r, r_r, s_a, r_a, s_s, r_s,
     s_c, r_c, s_y, r_y, s_m, r_m,
 ):
     p, d = lax.axis_index("pre"), lax.axis_index("dec")
     y, c = lax.div(p, 2), lax.rem(p, 2)
     x, z = lax.div(d, 4), lax.rem(d, 4)
-    vocab = lm.shape[1]
+    vocab = lm.shape[0]
 
     def at(xx, yy, zz, cc):
         return (2 * yy + cc, 4 * xx + zz)
@@ -50,6 +52,15 @@
             src_ref=src, dst_ref=dst, send_sem=ssem, recv_sem=rsem,
             device_id=device, device_id_type=MESH,
         ).start()
+
+    pending = []
+
+    def later(ref, sem):
+        pending.append(lambda: drain(ref, sem))
+
+    def finish():
+        for wait in pending:
+            wait()
 
     def signal(device):
         pl.semaphore_signal(barrier, inc=1, device_id=device, device_id_type=MESH)
@@ -65,9 +76,9 @@
     for i in (1, 2, 3):
         signal(at(turn(x, i), y, z, 1 - c))
         signal(at(x, y, turn(z, i), 1 - c))
-    for i, j in DEC:
-        signal(at(y, turn(y, i), turn(z, j), c))
-        signal(at(turn(x, i), turn(y, j), y, c))
+    for i in (1, 2, 3):
+        signal(at(y, turn(y, i), z, c))
+        signal(at(x, turn(y, i), y, c))
 
     @pl.when(x != y)
     def _():
@@ -79,7 +90,7 @@
 
     pl.semaphore_wait(
         barrier,
-        15 + 7 + 6 + 30 + (x != y).astype(jnp.int32) + (z != y).astype(jnp.int32),
+        15 + 7 + 6 + 6 + (x != y).astype(jnp.int32) + (z != y).astype(jnp.int32),
     )
 
     def group_of(axis, xx, yy, zz, cc):
@@ -103,33 +114,40 @@
             kbuf.at[k, :, pl.ds(64 * mine, 64), :],
             r_k.at[k],
         ).start()
-
-    QROWS = {"x": (0, 16), "y": (16, 32), "z": (48, 16)}
-    QSEM = {"x": 0, "y": 1, "z": 2}
-
-    def send_query(axis):
-        first, rows = QROWS[axis]
-        sem = QSEM[axis]
-        for i, j in DEC:
-            xx, zz = turn(x, i), turn(z, j)
+        later(kbuf.at[k, :, pl.ds(0, 448), :], s_k.at[k])
+
+    def along(axis, step):
+        return (turn(x, step), z) if axis == "x" else (x, turn(z, step))
+
+    def coordinate(axis):
+        return x if axis == "x" else z
+
+    def send_query(k):
+        axis = PAIRS[k]
+        block = qbuf.at[k, coordinate(FIRST[k]), coordinate(EARLY[k])]
+        for i in (1, 2, 3):
+            xx, zz = along(EARLY[k], i)
             send(
-                query.at[pl.ds(64 * group_of(axis, xx, y, zz, c) + first, rows)],
-                qbuf.at[d, pl.ds(first, rows), :],
-                s_q.at[sem], r_q.at[sem], at(xx, y, zz, c),
+                query.at[pl.ds(64 * group_of(axis, xx, y, zz, c) + 16 * k, 16)], block,
+                s_q.at[k], r_q.at[k], at(xx, y, zz, c),
             )
         pltpu.make_async_copy(
-            query.at[pl.ds(64 * group_of(axis, x, y, z, c) + first, rows)],
-            qbuf.at[d, pl.ds(first, rows), :],
-            r_q.at[sem],
+            query.at[pl.ds(64 * group_of(axis, x, y, z, c) + 16 * k, 16)], block, r_q.at[k]
         ).start()
-
-    send_cache(1)
-    send_query("y")
-    send_query("x")
-    send_query("z")
-    send_cache(0)
-    send_cache(3)
-    send_cache(2)
+        later(qbuf.at[k, 0, pl.ds(0, 3)], s_q.at[k])
+
+    def pass_query(k):
+        met = qbuf.at[k, coordinate(FIRST[k])]
+        drain(met, r_q.at[k])
+        for i in (1, 2, 3):
+            xx, zz = along(FIRST[k], i)
+            send(met, met, s_v.at[k], r_v.at[k], at(xx, y, zz, c))
+        later(qbuf.at[k, pl.ds(0, 3)], s_v.at[k])
+
+    for k in range(4):
+        send_query(k)
+    for k in (1, 0, 3, 2):
+        send_cache(k)
     loads = [
         pltpu.make_async_copy(query.at[pl.ds(64 * p, 64)], qown, l_w.at[0]),
         pltpu.make_async_copy(vw, vwv, l_w.at[1]),
@@ -139,6 +157,14 @@
     for load in loads:
         load.start()
 
+    def window(rows, n):
+        left = 384 * (n % 2)
+        block = rows[8 * (n // 2):8 * (n // 2) + 8]
+        return jnp.concatenate([block[:, left:left + 256], block[:, left + 256:left + 512]], axis=0)
+
+    for k in (1, 0, 3, 2):
+        pass_query(k)
+
     loads[0].wait()
     row = lax.broadcasted_iota(jnp.int32, (64, 64), 0)
     col = lax.broadcasted_iota(jnp.int32, (64, 64), 1)
@@ -147,10 +173,13 @@
     own = jnp.sum(qown[...].astype(jnp.float32) * new_rows, axis=1, keepdims=True) * SCALE
     to_slot = (slots[...] == row).astype(jnp.float32).astype(jnp.bfloat16)
     resid_slot = jnp.dot(to_slot, resid[...], preferred_element_type=jnp.float32)
+    for n in range(16):
+        resw[n] = window(resid_slot, n)
     ls[:, :, :, pl.ds(HALF - 128, 128)] = jnp.zeros((2, 4, 16, 128), jnp.bfloat16)
 
     spot = lax.broadcasted_iota(jnp.int32, (1, 512), 1)
     lane = lax.broadcasted_iota(jnp.int32, (128, EXTRA), 1)
+    lane16 = lax.broadcasted_iota(jnp.int32, (16, EXTRA), 1)
 
     def position(axis):
         slot, core, inner = spot >> 7, (spot >> 6) & 1, spot & 63
@@ -161,10 +190,11 @@
 
     def attend(k):
         axis = PAIRS[k]
+        drain(qbuf.at[k, pl.ds(0, 3)], r_v.at[k])
         drain(kbuf.at[k], r_k.at[k])
         spots = position(axis)
         group = group_of(axis, x, y, z, c)
-        both = qbuf[:, pl.ds(16 * k, 16), :].astype(jnp.float32).reshape(16, 2, 8, WIDTH)
+        both = qbuf[k].astype(jnp.float32).reshape(16, 2, 8, WIDTH)
         sums, extras = [], []
         for j in range(2):
             rows = both[:, j].reshape(128, WIDTH).astype(jnp.bfloat16)
@@ -186,19 +216,56 @@
             high = total.astype(jnp.bfloat16).astype(jnp.float32)
             extra = jnp.where(lane == 0, top, jnp.where(lane == 1, high, total - high))
             extras.append(extra.reshape(16, 8, EXTRA))
-        pout[k, :, :, pl.ds(0, KV_RANK)] = jnp.concatenate(sums, axis=1).astype(jnp.bfloat16)
-        pout[k, :, :, pl.ds(KV_RANK, EXTRA)] = jnp.concatenate(extras, axis=1).astype(jnp.bfloat16)
+        sums = jnp.concatenate(sums, axis=1).astype(jnp.bfloat16).reshape(4, 4, 16, KV_RANK)
+        extras = jnp.concatenate(extras, axis=1).astype(jnp.bfloat16).reshape(4, 4, 16, EXTRA)
+        for n in range(4):
+            pout[k, n, :, :, pl.ds(0, KV_RANK)] = sums[n]
+            pout[k, n, :, :, pl.ds(KV_RANK, EXTRA)] = extras[n]
+        for i in (1, 2, 3):
+            xx, zz = along(FIRST[k], i)
+            send(
+                pout.at[k, xx if FIRST[k] == "x" else zz], pmid.at[k, i - 1],
+                s_p.at[k], r_p.at[k], at(xx, y, zz, c),
+            )
+        later(pmid.at[k], s_p.at[k])
+
+    def joined(blocks, own=None):
+        extra = [block[..., KV_RANK:].astype(jnp.float32) for block in blocks]
+        tops = [part[..., 0:1] for part in extra]
+        top = functools.reduce(jnp.maximum, tops)
+        if own is not None:
+            top = jnp.maximum(top, own)
+        shrink = [jnp.exp(part - top) for part in tops]
+        total = sum((part[..., 1:2] + part[..., 2:3]) * by for part, by in zip(extra, shrink))
+        summed = sum(
+            block[..., :KV_RANK].astype(jnp.float32) * by for block, by in zip(blocks, shrink)
+        )
+        return top, total, summed
+
+    def join_first(k):
+        axis, first = PAIRS[k], FIRST[k]
+        drain(pmid.at[k], r_p.at[k])
+        for n in range(4):
+            blocks = [pout[k, coordinate(first), n]] + [pmid[k, i, n] for i in range(3)]
+            top, total, summed = joined(blocks)
+            high = total.astype(jnp.bfloat16).astype(jnp.float32)
+            extra = jnp.where(lane16 == 0, top, jnp.where(lane16 == 1, high, total - high))
+            pjoin[k, n, :, pl.ds(0, KV_RANK)] = summed.astype(jnp.bfloat16)
+            pjoin[k, n, :, pl.ds(KV_RANK, EXTRA)] = extra.astype(jnp.bfloat16)
         yy = {"x": x, "y": y, "z": z}[axis]
-        place = {"x": 4 * y + z, "y": d, "z": 4 * x + y}[axis]
-        for i, j in DEC:
-            xx, zz = turn(x, i), turn(z, j)
+        place = y if axis != "y" else (z if first == "x" else x)
+        here = z if first == "x" else x
+        for i in (1, 2, 3):
+            other = turn(here, i)
+            xx, zz = (x, other) if first == "x" else (other, z)
             send(
-                pout.at[k, 4 * xx + zz], pin.at[k, place],
-                s_p.at[k], r_p.at[k], at(xx, yy, zz, c),
+                pjoin.at[k, other], pin.at[k, place],
+                s_j.at[k], r_j.at[k], at(xx, yy, zz, c),
             )
+        later(pin.at[k, pl.ds(0, 3)], s_j.at[k])
 
         def keep():
-            pltpu.make_async_copy(pout.at[k, d], pin.at[k, place], r_p.at[k]).start()
+            pltpu.make_async_copy(pjoin.at[k, here], pin.at[k, place], r_j.at[k]).start()
 
         if axis == "y":
             keep()
@@ -208,35 +275,34 @@
             @pl.when(yy != y)
             def _():
                 send(
-                    pout.at[k, d], pin.at[k, place],
-                    s_p.at[k], r_p.at[k], at(x, yy, z, c),
+                    pjoin.at[k, here], pin.at[k, place],
+                    s_j.at[k], r_j.at[k], at(x, yy, z, c),
                 )
 
-    drain(qbuf.at[:, pl.ds(16, 32), :], r_q.at[1])
+            def left():
+                pl.when(yy != y)(lambda: drain(pin.at[k, 0], s_j.at[k]))
+
+            pending.append(left)
+
     attend(1)
-    drain(qbuf.at[:, pl.ds(0, 16), :], r_q.at[0])
     attend(0)
-    drain(qbuf.at[:, pl.ds(48, 16), :], r_q.at[2])
+    join_first(1)
     attend(3)
+    join_first(0)
     attend(2)
+    join_first(3)
+    join_first(2)
 
     for k in (1, 0, 3, 2):
-        drain(pin.at[k], r_p.at[k])
-        extra = pin[k, :, :, pl.ds(KV_RANK, EXTRA)].astype(jnp.float32)
-        tops = extra[:, :, 0:1]
-        totals = extra[:, :, 1:2] + extra[:, :, 2:3]
+        drain(pin.at[k], r_j.at[k])
         own_k = own[16 * k:16 * k + 16]
-        top = jnp.maximum(jnp.max(tops, axis=0), own_k)
-        shrink = jnp.exp(tops - top[None])
+        top, total, summed = joined([pin[k, n] for n in range(4)], own_k)
         own_weight = jnp.exp(own_k - top)
-        total = jnp.sum(totals * shrink, axis=0) + own_weight
-        summed = (
+        summed = summed + (
             own_weight.astype(jnp.bfloat16).astype(jnp.float32)
             * new_rows[16 * k:16 * k + 16, :KV_RANK]
         )
-        for s in range(16):
-            summed = summed + shrink[s] * pin[k, s, :, pl.ds(0, KV_RANK)].astype(jnp.float32)
-        summed = summed / total
+        summed = summed / (total + own_weight)
         for b in range(KV_RANK // 128):
             lat[b, pl.ds(16 * k, 16), :] = summed[:, 128 * b:128 * b + 128]
 
@@ -253,12 +319,13 @@
     hv[p] = packed.astype(jnp.bfloat16)
     for n, (i, j) in enumerate(PRE):
         send(hv.at[p], hv.at[p], s_h.at[n], r_h.at[n], at(x, turn(y, i), z, lax.rem(c + j, 2)))
+        later(hv.at[0], s_h.at[n])
     loads[2].wait()
     for n in range(7):
         drain(hv.at[0], r_h.at[n])
 
     heads = hv[...].astype(jnp.float32).reshape(8, 2, 8, KV_RANK)
-    part = resid_slot * jnp.where(d == 0, 1.0, 0.0)
+    part = jnp.zeros((64, owv.shape[1]), jnp.float32)
     for half in range(2):
         rows = heads[:, half].reshape(64, KV_RANK).astype(jnp.bfloat16)
         rows = jnp.dot(to_slot, rows, preferred_element_type=jnp.float32).astype(jnp.bfloat16)
@@ -266,28 +333,55 @@
             rows, owv[pl.ds(KV_RANK * half, KV_RANK), :], preferred_element_type=jnp.float32
         )
     for s in range(16):
-        rss[s] = part[4 * s:4 * s + 4]
+        rss[s] = window(part, s).astype(jnp.bfloat16)
     for n, (i, j) in enumerate(DEC):
         xx, zz = turn(x, i), turn(z, j)
         send(rss.at[4 * xx + zz], rsr.at[n], s_r.at[0], r_r.at[0], at(xx, y, zz, c))
+    later(rsr, s_r.at[0])
     drain(rsr, r_r.at[0])
-    hidden4 = rss[d]
+    hidden = resw[d] + rss[d].astype(jnp.float32)
     for n in range(15):
-        hidden4 = hidden4 + rsr[n]
-    hsl[d] = hidden4
+        hidden = hidden + rsr[n].astype(jnp.float32)
+    odd = lax.rem(d, 2) == 1
+    gains = jnp.broadcast_to(gain[...].astype(jnp.float32).reshape(1, -1), (8, owv.shape[1]))
+    scaled = hidden * jnp.where(odd, window(gains, 1), window(gains, 0))
+    twice = (
+        (lax.broadcasted_iota(jnp.int32, (16, 256), 0) < 8)
+        & (lax.broadcasted_iota(jnp.int32, (16, 256), 1) < 128)
+        & odd
+    )
+    squares = jnp.sum(jnp.where(twice, 0.0, hidden * hidden), axis=1, keepdims=True)
+    squares = squares + jnp.concatenate([squares[8:], squares[:8]], axis=0)
+    first = squares.astype(jnp.bfloat16).astype(jnp.float32)
+    second = (squares - first).astype(jnp.bfloat16).astype(jnp.float32)
+    third = squares - first - second
+    agb[d, :, pl.ds(0, 256)] = scaled.astype(jnp.bfloat16)
+    agb[d, :, pl.ds(256, 128)] = jnp.where(
+        lane16 == 0, first, jnp.where(lane16 == 1, second, third)
+    ).astype(jnp.bfloat16)
     for n, (i, j) in enumerate(DEC):
-        send(hsl.at[d], hsl.at[d], s_a.at[n], r_a.at[n], at(turn(x, i), y, turn(z, j), c))
+        send(agb.at[d], agb.at[d], s_a.at[n], r_a.at[n], at(turn(x, i), y, turn(z, j), c))
+        later(agb.at[0], s_a.at[n])
     for n in range(15):
-        drain(hsl.at[0], r_a.at[n])
-    for s in range(16):
-        hid[pl.ds(4 * s, 4), :] = hsl[s]
-    hidden = hid[...]
-    squares = jnp.sum(hidden * hidden, axis=1, keepdims=True)
-    sqs[...] = jnp.broadcast_to(squares, (64, 128)).reshape(8, 8, 128)
+        drain(agb.at[0], r_a.at[n])
+    gathered = agb[...].astype(jnp.float32).reshape(8, 2, 2, 8, 384)
+    squares = sum(
+        gathered[:, h, 0, :, 256 + n:257 + n] for h in range(2) for n in range(3)
+    )
+    sqs[...] = jnp.broadcast_to(squares, (8, 8, 128))
     for n, (i, j) in enumerate(PRE):
         yy, cc = turn(y, i), lax.rem(c + j, 2)
         send(sqs.at[2 * yy + cc], sqr.at[n], s_s.at[0], r_s.at[0], at(x, yy, z, cc))
-    scaled = (hidden * gain[...].astype(jnp.float32)).astype(jnp.bfloat16)
+    later(sqr, s_s.at[0])
+    scaled = jnp.concatenate(
+        [
+            gathered[:, 0, 0, :, 0:256].reshape(64, 256),
+            gathered[:, 0, 1, :, 0:256].reshape(64, 256),
+            gathered[:, 1, 0, :, 128:256].reshape(64, 128),
+            gathered[:, 1, 1, :, 0:256].reshape(64, 256),
+        ],
+        axis=1,
+    ).astype(jnp.bfloat16)
 
     wide = HALF // CHUNKS
 
@@ -303,14 +397,16 @@
                 ls.at[c, yy, :, lanes], lb.at[step - 1, :, lanes],
                 s_y.at[i], r_y.at[i], at(x, yy, z, c),
             )
+        later(lb.at[:, :, lanes], s_y.at[i])
 
     loads[3].wait()
     for i in range(CHUNKS):
         for half in range(2):
             start = HALF * half + wide * i
             count = min(wide, vocab - start)
-            product = jnp.dot(
-                scaled, lmv[:, pl.ds(start, count)], preferred_element_type=jnp.float32
+            product = lax.dot_general(
+                scaled, lmv[pl.ds(start, count), :], (((1,), (1,)), ((), ())),
+                preferred_element_type=jnp.float32,
             ).reshape(8, 8, count).astype(jnp.bfloat16)
             for q in range(8):
                 ls[q % 2, q // 2, pl.ds(8 * half, 8), pl.ds(wide * i, count)] = product[q]
@@ -319,6 +415,7 @@
             ls.at[1 - c, :, :, lanes], lr.at[:, :, lanes],
             s_c.at[i], r_c.at[i], at(x, y, z, 1 - c),
         )
+        later(lr.at[:, :, lanes], s_c.at[i])
         if i > 0:
             join_cores(i - 1)
     join_cores(CHUNKS - 1)
@@ -355,6 +452,7 @@
     sms[...] = mine
     for n, (i, j) in enumerate(DEC):
         send(sms, smr.at[n], s_m.at[0], r_m.at[0], at(turn(x, i), y, turn(z, j), c))
+    later(smr, s_m.at[0])
     drain(smr, r_m.at[0])
     others = smr[...]
     best = jnp.maximum(jnp.max(others[:, :, 0:1], axis=0), top)
@@ -365,30 +463,12 @@
     normalizer = best + jnp.log(total)
     out[:, pl.ds(0, HALF)] = low - normalizer
     out[:, pl.ds(HALF, vocab - HALF)] = (high - normalizer)[:, : vocab - HALF]
-    tgt[...] = jnp.broadcast_to(picked - normalizer, (8, 128))
-
-    for k in range(4):
-        drain(kbuf.at[k, :, pl.ds(0, 448), :], s_k.at[k])
-        drain(pin.at[k, pl.ds(0, 15)], s_p.at[k])
-        if PAIRS[k] != "y":
-
-            @pl.when({"x": x, "z": z}[PAIRS[k]] != y)
-            def _():
-                drain(pin.at[k, 0], s_p.at[k])
-
-    for axis in "xyz":
-        first, rows = QROWS[axis]
-        drain(qbuf.at[pl.ds(0, 15), pl.ds(first, rows), :], s_q.at[QSEM[axis]])
-    for n in range(7):
-        drain(hv.at[0], s_h.at[n])
-    drain(rsr, s_r.at[0])
-    for n in range(15):
-        drain(hsl.at[0], s_a.at[n])
-    drain(sqr, s_s.at[0])
-    for i in range(CHUNKS):
-        drain(lr.at[:, :, pl.ds(wide * i, wide)], s_c.at[i])
-        drain(lb.at[:, :, pl.ds(wide * i, wide)], s_y.at[i])
-    drain(smr, s_m.at[0])
+    square = lax.broadcasted_iota(jnp.int32, (8, 8), 0) == lax.broadcasted_iota(
+        jnp.int32, (8, 8), 1
+    )
+    tgt[...] = jnp.sum(jnp.where(square, picked - normalizer, 0.0), axis=0, keepdims=True)
+
+    finish()
 
 
 def body(
@@ -405,26 +485,28 @@
         kernel,
         out_shape=(
             jax.ShapeDtypeStruct((8, vocab), f32),
-            jax.ShapeDtypeStruct((8, 128), f32),
+            jax.ShapeDtypeStruct((1, 8), f32),
         ),
         in_specs=[smem, anywhere, anywhere, vmem, vmem, vmem, vmem, vmem,
                   anywhere, anywhere, anywhere],
         out_specs=(vmem, vmem),
         scratch_shapes=[
             pltpu.VMEM((4, 2, 512, WIDTH), bf16),
-            pltpu.VMEM((16, 64, WIDTH), bf16),
-            pltpu.VMEM((4, 16, 16, KV_RANK + EXTRA), bf16),
-            pltpu.VMEM((4, 16, 16, KV_RANK + EXTRA), bf16),
+            pltpu.VMEM((4, 4, 4, 16, WIDTH), bf16),
+            pltpu.VMEM((4, 4, 4, 16, KV_RANK + EXTRA), bf16),
+            pltpu.VMEM((4, 4, 16, KV_RANK + EXTRA), bf16),
+            pltpu.VMEM((4, 3, 4, 16, KV_RANK + EXTRA), bf16),
+            pltpu.VMEM((4, 4, 16, KV_RANK + EXTRA), bf16),
             pltpu.VMEM((8, KV_RANK, VHEAD), bf16),
             pltpu.VMEM((1024, columns), bf16),
-            pltpu.VMEM((columns, vocab), bf16),
+            pltpu.VMEM((vocab, columns), bf16),
             pltpu.VMEM((64, WIDTH), bf16),
             pltpu.VMEM((KV_RANK // 128, 64, 128), f32),
             pltpu.VMEM((8, 16, 512), bf16),
-            pltpu.VMEM((16, 4, columns), f32),
-            pltpu.VMEM((15, 4, columns), f32),
-            pltpu.VMEM((16, 4, columns), f32),
-            pltpu.VMEM((64, columns), f32),
+            pltpu.VMEM((16, 16, 256), f32),
+            pltpu.VMEM((16, 16, 256), bf16),
+            pltpu.VMEM((15, 16, 256), bf16),
+            pltpu.VMEM((16, 16, 384), bf16),
             pltpu.VMEM((8, 8, 128), f32),
             pltpu.VMEM((7, 8, 128), f32),
             pltpu.VMEM((2, 4, 16, HALF), bf16),
@@ -432,7 +514,8 @@
             pltpu.VMEM((3, 16, HALF), bf16),
             pltpu.VMEM((8, 128), f32),
             pltpu.VMEM((15, 8, 128), f32),
-            dma((4,)), dma((4,)), dma((3,)), dma((3,)), dma((4,)), dma((4,)), dma((4,)),
+            dma((4,)), dma((4,)), dma((4,)), dma((4,)), dma((4,)), dma((4,)), dma((4,)), dma((4,)), dma((4,)), dma((4,)),
+            dma((4,)),
             dma((7,)), dma((7,)), dma((1,)), dma((1,)), dma((15,)), dma((15,)),
             dma((1,)), dma((1,)), dma((CHUNKS,)), dma((CHUNKS,)), dma((CHUNKS,)),
             dma((CHUNKS,)), dma((1,)), dma((1,)),
@@ -449,12 +532,12 @@
         slot_of.reshape(1, -1),
         token_ids.reshape(1, -1),
         residual,
-        norm_gain.reshape(1, -1),
+        norm_gain,
         latent_value_weight,
         out_weight,
-        lm_weight,
-    )
-    return logprobs, target[:, 0]
+        lm_weight.T,
+    )
+    return logprobs, target.reshape(8)
 
 
 def solution(mesh):

time: 125 us -> 91 us (0.73)
  local copies, waits for them, and re-layouts: 23.5 us -> 2.8 us
  Pallas kernels: 100 us -> 87.4 us
    unnamed x2, local copies, waits for them, and re-layouts: 21 us -> 2.8 us
    pallas_call x1, Pallas kernels: 100 us -> 87.4 us  [body(): pl.pallas_call(kernel, out_shape=(jax.ShapeDtypeStruct((8, vocab), f32),...]
    slice x1 -> x0, local copies, waits for them, and re-layouts: 1.3 us -> none  [body(): return (logprobs, target[:, 0])]
    reshape x1 -> x0, local copies, waits for them, and re-layouts: 1.26 us -> none  [body(): norm_gain.reshape(1, -1)]
where the time goes in v2:
time: 91 us; the launch traced here: 90.8 us
  Pallas kernels  87.4 us (96%)
  local copies, waits for them, and re-layouts  2.8 us (3%)
    pallas_call x1, Pallas kernels, body(): pl.pallas_call(kernel, out_shape=(jax.ShapeDtypeStruct((8, vocab), f32),...  87.4 us
    unnamed x2, local copies, waits for them, and re-layouts  2.8 us

profile of v2, /device:TPU:0, one launch (start us, length us, event | category | flops | bytes accessed | tf_op | source)
XLA Modules:
  0.0 90.8 jit_solution(12186684874525620285)
XLA Ops:
  0.6 87.4 %decode_step.1 = (f32[8,8080]{1,0:T(8,128)}, f32[1,8]{1,0:T(1,128)}) custom-call(s32[64]{0:T(128)} %lens.1, bf16[64,64,576]{2,1,0:T(8,128)(2,1)} %cache.1, bf16[512,576]{1,0:T(8,128)(2,1)} %bitcast.6, bf16[64,576]{1,0:T(8,128)(2,1)} %newl.1, s32[1,64]{1,0:T(1,128)} %bitcast.7, s32[1,64]{1,0:T(1,128)} %bitcast.8, bf16[64,896]{1,0:T(8,128)(2,1)} %resid.1, ...), custom_call_target="tpu_custom_call" | custom-call | tf_op jit(solution)/shard_map/decode_step/pallas_call | solution.py:484
  88.0 1.7 %copy.15 = f32[8,8080]{1,0:T(8,128)} copy(f32[8,8080]{1,0:T(8,128)} %get-tuple-element.8) | data formatting | bytes 517120
  89.7 1.1 %copy.16 = f32[8]{0:T(128)} copy(f32[8]{0:T(128)} %bitcast.9) | data formatting | bytes 64

commit v3 on v2

--- a/solution.py
+++ b/solution.py
@@ -31,9 +31,9 @@
 def kernel(
     lens, cache, query, newl, slots, toks, resid, gain, vw, ow, lm,
     out, tgt,
-    kbuf, qbuf, pout, pjoin, pmid, pin, vwv, owv, lmv, qown, lat, hv, resw, rss, rsr, agb,
+    kbuf, raw, rope, krope, qbuf, pout, pjoin, pmid, pin, vwv, owv, lmv, qown, lat, hv, resw, rss, rsr, agb,
     sqs, sqr, ls, lr, lb, sms, smr,
-    s_k, r_k, s_q, r_q, s_v, r_v, s_p, r_p, s_j, r_j, l_w, s_h, r_h, s_r, r_r, s_a, r_a, s_s, r_s,
+    s_k, r_k, s_o, r_o, s_q, r_q, s_v, r_v, s_p, r_p, s_j, r_j, l_w, s_h, r_h, s_r, r_r, s_a, r_a, s_s, r_s,
     s_c, r_c, s_y, r_y, s_m, r_m,
 ):
     p, d = lax.axis_index("pre"), lax.axis_index("dec")
@@ -88,6 +88,32 @@
     def _():
         signal(at(x, y, y, c))
 
+    loads = [
+        pltpu.make_async_copy(query.at[pl.ds(64 * p, 64)], qown, l_w.at[0]),
+        pltpu.make_async_copy(vw, vwv, l_w.at[1]),
+        pltpu.make_async_copy(ow, owv, l_w.at[2]),
+        pltpu.make_async_copy(lm, lmv, l_w.at[3]),
+        pltpu.make_async_copy(cache.at[:, :, pl.ds(KV_RANK, ROPE)], raw, l_w.at[4]),
+    ]
+    for n in (4, 0, 1, 2):
+        loads[n].start()
+    def half(j):
+        down = lax.broadcasted_iota(jnp.int32, (ROPE, 2 * ROPE), 0) + ROPE * j
+        right = lax.broadcasted_iota(jnp.int32, (ROPE, 2 * ROPE), 1)
+        return (down == right).astype(jnp.float32).astype(jnp.bfloat16)
+
+    halves = [half(0), half(1)]
+    loads[4].wait()
+    for n in range(4):
+        keys = raw[pl.ds(16 * n, 16)].reshape(8, 2, 64, ROPE)
+        both = sum(
+            jnp.dot(
+                keys[:, j].reshape(512, ROPE), halves[j], preferred_element_type=jnp.float32
+            )
+            for j in range(2)
+        )
+        rope[pl.ds(8 * n, 8)] = both.astype(jnp.bfloat16).reshape(8, 64, 2 * ROPE)
+
     pl.semaphore_wait(
         barrier,
         15 + 7 + 6 + 6 + (x != y).astype(jnp.int32) + (z != y).astype(jnp.int32),
@@ -96,7 +122,7 @@
     def group_of(axis, xx, yy, zz, cc):
         return 2 * {"x": xx, "y": yy, "z": zz}[axis] + cc
 
-    def send_cache(k):
+    def send_cache(k, source, target, ssem, rsem):
         axis = PAIRS[k]
         mine = group_of(axis, x, y, z, c)
         for i, j in PRE:
@@ -105,16 +131,28 @@
             zz = turn(z, i) if axis == "z" else z
             cc = lax.rem(c + j, 2)
             send(
-                cache.at[pl.ds(8 * group_of(axis, xx, yy, zz, cc) + 2 * k, 2)],
-                kbuf.at[k, :, pl.ds(64 * mine, 64), :],
-                s_k.at[k], r_k.at[k], at(xx, yy, zz, cc),
-            )
-        pltpu.make_async_copy(
-            cache.at[pl.ds(8 * mine + 2 * k, 2)],
-            kbuf.at[k, :, pl.ds(64 * mine, 64), :],
-            r_k.at[k],
-        ).start()
+                source(group_of(axis, xx, yy, zz, cc)), target(mine),
+                ssem.at[k], rsem.at[k], at(xx, yy, zz, cc),
+            )
+        pltpu.make_async_copy(source(mine), target(mine), rsem.at[k]).start()
+
+    def send_latents(k):
+        send_cache(
+            k,
+            lambda group: cache.at[pl.ds(8 * group + 2 * k, 2), :, pl.ds(0, KV_RANK)],
+            lambda mine: kbuf.at[k, :, pl.ds(64 * mine, 64), :],
+            s_k, r_k,
+        )
         later(kbuf.at[k, :, pl.ds(0, 448), :], s_k.at[k])
+
+    def send_ropes(k):
+        send_cache(
+            k,
+            lambda group: rope.at[4 * group + k],
+            lambda mine: krope.at[k, pl.ds(64 * mine, 64), :],
+            s_o, r_o,
+        )
+        later(krope.at[k, pl.ds(0, 448), :], s_o.at[k])
 
     def along(axis, step):
         return (turn(x, step), z) if axis == "x" else (x, turn(z, step))
@@ -144,26 +182,22 @@
             send(met, met, s_v.at[k], r_v.at[k], at(xx, y, zz, c))
         later(qbuf.at[k, pl.ds(0, 3)], s_v.at[k])
 
+    send_latents(1)
     for k in range(4):
         send_query(k)
+    send_ropes(1)
+    for k in (0, 3, 2):
+        send_latents(k)
+        send_ropes(k)
+    loads[3].start()
+
     for k in (1, 0, 3, 2):
-        send_cache(k)
-    loads = [
-        pltpu.make_async_copy(query.at[pl.ds(64 * p, 64)], qown, l_w.at[0]),
-        pltpu.make_async_copy(vw, vwv, l_w.at[1]),
-        pltpu.make_async_copy(ow, owv, l_w.at[2]),
-        pltpu.make_async_copy(lm, lmv, l_w.at[3]),
-    ]
-    for load in loads:
-        load.start()
+        pass_query(k)
 
     def window(rows, n):
         left = 384 * (n % 2)
         block = rows[8 * (n // 2):8 * (n // 2) + 8]
         return jnp.concatenate([block[:, left:left + 256], block[:, left + 256:left + 512]], axis=0)
-
-    for k in (1, 0, 3, 2):
-        pass_query(k)
 
     loads[0].wait()
     row = lax.broadcasted_iota(jnp.int32, (64, 64), 0)
@@ -191,16 +225,31 @@
     def attend(k):
         axis = PAIRS[k]
         drain(qbuf.at[k, pl.ds(0, 3)], r_v.at[k])
-        drain(kbuf.at[k], r_k.at[k])
         spots = position(axis)
         group = group_of(axis, x, y, z, c)
         both = qbuf[k].astype(jnp.float32).reshape(16, 2, 8, WIDTH)
+        queries = []
+        for j in range(2):
+            rows = both[:, j].reshape(128, WIDTH)
+            turned = jnp.dot(
+                rows[:, KV_RANK:].astype(jnp.bfloat16), halves[j],
+                preferred_element_type=jnp.float32,
+            )
+            queries.append((rows[:, :KV_RANK].astype(jnp.bfloat16), turned.astype(jnp.bfloat16)))
+        drain(krope.at[k], r_o.at[k])
+        drain(kbuf.at[k], r_k.at[k])
         sums, extras = [], []
         for j in range(2):
-            rows = both[:, j].reshape(128, WIDTH).astype(jnp.bfloat16)
             keys = kbuf[k, j]
-            scores = lax.dot_general(
-                rows, keys, (((1,), (1,)), ((), ())), preferred_element_type=jnp.float32
+            scores = (
+                lax.dot_general(
+                    queries[j][0], keys, (((1,), (1,)), ((), ())),
+                    preferred_element_type=jnp.float32,
+                )
+                + lax.dot_general(
+                    queries[j][1], krope[k], (((1,), (1,)), ((), ())),
+                    preferred_element_type=jnp.float32,
+                )
             ) * SCALE
             scores = jnp.where(spots < lens[8 * group + 2 * k + j], scores, FILL)
             top = jnp.max(scores, axis=1, keepdims=True)
@@ -209,7 +258,7 @@
             total = jnp.sum(weights, axis=1, keepdims=True)
             sums.append(
                 jnp.dot(
-                    weights.astype(jnp.bfloat16), keys[:, :KV_RANK],
+                    weights.astype(jnp.bfloat16), keys,
                     preferred_element_type=jnp.float32,
                 ).reshape(16, 8, KV_RANK)
             )
@@ -284,19 +333,11 @@
 
             pending.append(left)
 
-    attend(1)
-    attend(0)
-    join_first(1)
-    attend(3)
-    join_first(0)
-    attend(2)
-    join_first(3)
-    join_first(2)
-
-    for k in (1, 0, 3, 2):
+    def join_last(k):
         drain(pin.at[k], r_j.at[k])
+        blocks = [pin[k, n] for n in range(4)]
         own_k = own[16 * k:16 * k + 16]
-        top, total, summed = joined([pin[k, n] for n in range(4)], own_k)
+        top, total, summed = joined(blocks, own_k)
         own_weight = jnp.exp(own_k - top)
         summed = summed + (
             own_weight.astype(jnp.bfloat16).astype(jnp.float32)
@@ -305,6 +346,19 @@
         summed = summed / (total + own_weight)
         for b in range(KV_RANK // 128):
             lat[b, pl.ds(16 * k, 16), :] = summed[:, 128 * b:128 * b + 128]
+
+    attend(1)
+    attend(0)
+    join_first(1)
+    attend(3)
+    join_first(0)
+    attend(2)
+    join_first(3)
+    for k in (1, 0):
+        join_last(k)
+    join_first(2)
+    for k in (3, 2):
+        join_last(k)
 
     loads[1].wait()
     values = []
@@ -491,7 +545,10 @@
                   anywhere, anywhere, anywhere],
         out_specs=(vmem, vmem),
         scratch_shapes=[
-            pltpu.VMEM((4, 2, 512, WIDTH), bf16),
+            pltpu.VMEM((4, 2, 512, KV_RANK), bf16),
+            pltpu.VMEM((64, 64, ROPE), bf16),
+            pltpu.VMEM((32, 64, 2 * ROPE), bf16),
+            pltpu.VMEM((4, 512, 2 * ROPE), bf16),
             pltpu.VMEM((4, 4, 4, 16, WIDTH), bf16),
             pltpu.VMEM((4, 4, 4, 16, KV_RANK + EXTRA), bf16),
             pltpu.VMEM((4, 4, 16, KV_RANK + EXTRA), bf16),
@@ -514,8 +571,8 @@
             pltpu.VMEM((3, 16, HALF), bf16),
             pltpu.VMEM((8, 128), f32),
             pltpu.VMEM((15, 8, 128), f32),
-            dma((4,)), dma((4,)), dma((4,)), dma((4,)), dma((4,)), dma((4,)), dma((4,)), dma((4,)), dma((4,)), dma((4,)),
-            dma((4,)),
+            dma((4,)), dma((4,)), dma((4,)), dma((4,)), dma((4,)), dma((4,)), dma((4,)), dma((4,)), dma((4,)), dma((4,)), dma((4,)), dma((4,)),
+            dma((5,)),
             dma((7,)), dma((7,)), dma((1,)), dma((1,)), dma((15,)), dma((15,)),
             dma((1,)), dma((1,)), dma((CHUNKS,)), dma((CHUNKS,)), dma((CHUNKS,)),
             dma((CHUNKS,)), dma((1,)), dma((1,)),

time: 91 us -> 88.2 us (0.969)
  Pallas kernels: 87.4 us -> 84.5 us
    pallas_call x1, Pallas kernels: 87.4 us -> 84.5 us  [body(): pl.pallas_call(kernel, out_shape=(jax.ShapeDtypeStruct((8, vocab), f32),...]
where the time goes in v3:
time: 88.2 us; the launch traced here: 88 us
  Pallas kernels  84.5 us (96%)
  local copies, waits for them, and re-layouts  2.8 us (3%)
    pallas_call x1, Pallas kernels, body(): pl.pallas_call(kernel, out_shape=(jax.ShapeDtypeStruct((8, vocab), f32),...  84.5 us
    unnamed x2, local copies, waits for them, and re-layouts  2.8 us

profile of v3, /device:TPU:0, one launch (start us, length us, event | category | flops | bytes accessed | tf_op | source)
XLA Modules:
  0.0 88.0 jit_solution(6382489456208732033)
XLA Ops:
  0.6 84.5 %decode_step.1 = (f32[8,8080]{1,0:T(8,128)}, f32[1,8]{1,0:T(1,128)}) custom-call(s32[64]{0:T(128)} %lens.1, bf16[64,64,576]{2,1,0:T(8,128)(2,1)} %cache.1, bf16[512,576]{1,0:T(8,128)(2,1)} %bitcast.6, bf16[64,576]{1,0:T(8,128)(2,1)} %newl.1, s32[1,64]{1,0:T(1,128)} %bitcast.7, s32[1,64]{1,0:T(1,128)} %bitcast.8, bf16[64,896]{1,0:T(8,128)(2,1)} %resid.1, ...), custom_call_target="tpu_custom_call" | custom-call | tf_op jit(solution)/shard_map/decode_step/pallas_call | solution.py:538
  85.2 1.7 %copy.15 = f32[8,8080]{1,0:T(8,128)} copy(f32[8,8080]{1,0:T(8,128)} %get-tuple-element.8) | data formatting | bytes 517120
  86.9 1.1 %copy.16 = f32[8]{0:T(128)} copy(f32[8]{0:T(128)} %bitcast.9) | data formatting | bytes 64

commit v4 on v3

--- a/solution.py
+++ b/solution.py
@@ -20,6 +20,8 @@
 CHUNKS = 4
 
 PAIRS = ("x", "y", "y", "z")
+FIRST_PAIR = 1
+LAST = 2
 EARLY = ("x", "z", "x", "z")
 FIRST = ("z", "x", "z", "x")
 
@@ -29,9 +31,9 @@
 
 
 def kernel(
-    lens, cache, query, newl, slots, toks, resid, gain, vw, ow, lm,
-    out, tgt,
-    kbuf, raw, rope, krope, qbuf, pout, pjoin, pmid, pin, vwv, owv, lmv, qown, lat, hv, resw, rss, rsr, agb,
+    lens_in, cache, query, newl_in, slots_in, toks_in, resid_in, gain_in, vw, ow, lm,
+    out, tail,
+    lens, newl, slots, toks, resid, gain, raws, kbuf, raw, rope, krope, qbuf, pout, pjoin, pmid, pin, vwv, owv, lmv, qown, lat, hv, resw, rss, rsr, agb,
     sqs, sqr, ls, lr, lb, sms, smr,
     s_k, r_k, s_o, r_o, s_q, r_q, s_v, r_v, s_p, r_p, s_j, r_j, l_w, s_h, r_h, s_r, r_r, s_a, r_a, s_s, r_s,
     s_c, r_c, s_y, r_y, s_m, r_m,
@@ -53,10 +55,15 @@
             device_id=device, device_id_type=MESH,
         ).start()
 
-    pending = []
+    pending, known = [], set()
 
     def later(ref, sem):
         pending.append(lambda: drain(ref, sem))
+
+    def once(key, wait):
+        if key not in known:
+            known.add(key)
+            pending.append(wait)
 
     def finish():
         for wait in pending:
@@ -68,6 +75,13 @@
     DEC = [(i, j) for i in range(4) for j in range(4) if (i, j) != (0, 0)]
     PRE = [(i, j) for i in range(4) for j in range(2) if (i, j) != (0, 0)]
 
+    loads = [
+        pltpu.make_async_copy(query.at[pl.ds(64 * p, 64)], qown, l_w.at[0]),
+        pltpu.make_async_copy(vw, vwv, l_w.at[1]),
+        pltpu.make_async_copy(ow, owv, l_w.at[2]),
+        pltpu.make_async_copy(lm, lmv, l_w.at[3]),
+        pltpu.make_async_copy(cache.at[:, :, pl.ds(KV_RANK, ROPE)], raw, l_w.at[4]),
+    ]
     barrier = pltpu.get_barrier_semaphore()
     for i, j in DEC:
         signal(at(turn(x, i), y, turn(z, j), c))
@@ -88,31 +102,19 @@
     def _():
         signal(at(x, y, y, c))
 
-    loads = [
-        pltpu.make_async_copy(query.at[pl.ds(64 * p, 64)], qown, l_w.at[0]),
-        pltpu.make_async_copy(vw, vwv, l_w.at[1]),
-        pltpu.make_async_copy(ow, owv, l_w.at[2]),
-        pltpu.make_async_copy(lm, lmv, l_w.at[3]),
-        pltpu.make_async_copy(cache.at[:, :, pl.ds(KV_RANK, ROPE)], raw, l_w.at[4]),
+    small = [
+        pltpu.make_async_copy(src, dst, l_w.at[5 + n])
+        for n, (src, dst) in enumerate([
+            (newl_in, newl), (slots_in, slots), (toks_in, toks), (resid_in, resid),
+            (gain_in, gain), (lens_in, lens),
+        ])
     ]
-    for n in (4, 0, 1, 2):
-        loads[n].start()
-    def half(j):
-        down = lax.broadcasted_iota(jnp.int32, (ROPE, 2 * ROPE), 0) + ROPE * j
-        right = lax.broadcasted_iota(jnp.int32, (ROPE, 2 * ROPE), 1)
-        return (down == right).astype(jnp.float32).astype(jnp.bfloat16)
-
-    halves = [half(0), half(1)]
-    loads[4].wait()
-    for n in range(4):
-        keys = raw[pl.ds(16 * n, 16)].reshape(8, 2, 64, ROPE)
-        both = sum(
-            jnp.dot(
-                keys[:, j].reshape(512, ROPE), halves[j], preferred_element_type=jnp.float32
-            )
-            for j in range(2)
-        )
-        rope[pl.ds(8 * n, 8)] = both.astype(jnp.bfloat16).reshape(8, 64, 2 * ROPE)
+    loads[4].start()
+    loads[0].start()
+    for load in small:
+        load.start()
+    loads[1].start()
+    loads[2].start()
 
     pl.semaphore_wait(
         barrier,
@@ -136,14 +138,28 @@
             )
         pltpu.make_async_copy(source(mine), target(mine), rsem.at[k]).start()
 
-    def send_latents(k):
-        send_cache(
-            k,
-            lambda group: cache.at[pl.ds(8 * group + 2 * k, 2), :, pl.ds(0, KV_RANK)],
-            lambda mine: kbuf.at[k, :, pl.ds(64 * mine, 64), :],
-            s_k, r_k,
-        )
-        later(kbuf.at[k, :, pl.ds(0, 448), :], s_k.at[k])
+    def send_latents(k, core):
+        axis = PAIRS[k]
+        target = kbuf.at[k, :, pl.ds(64 * group_of(axis, x, y, z, c), 64), :]
+
+        def source(xx, yy, zz, cc):
+            first = 8 * group_of(axis, xx, yy, zz, cc) + 2 * k
+            return cache.at[pl.ds(first, 2), :, pl.ds(0, KV_RANK)]
+
+        for i in (1, 2, 3):
+            xx = turn(x, i) if axis == "x" else x
+            yy = turn(y, i) if axis == "y" else y
+            zz = turn(z, i) if axis == "z" else z
+            send(
+                source(xx, yy, zz, core), target, s_k.at[k + 4 * core], r_k.at[k],
+                at(xx, yy, zz, core),
+            )
+        if core == 0:
+            send(source(x, y, z, 1 - c), target, s_k.at[k], r_k.at[k], at(x, y, z, 1 - c))
+            pltpu.make_async_copy(source(x, y, z, c), target, r_k.at[k]).start()
+
+    def latents_left(k, core):
+        drain(kbuf.at[k, :, pl.ds(0, 192 if core else 256), :], s_k.at[k + 4 * core])
 
     def send_ropes(k):
         send_cache(
@@ -162,16 +178,18 @@
 
     def send_query(k):
         axis = PAIRS[k]
-        block = qbuf.at[k, coordinate(FIRST[k]), coordinate(EARLY[k])]
+        met = qbuf.at[k, coordinate(FIRST[k])]
+        rows = query.at[pl.ds(64 * group_of(axis, x, y, z, c) + 16 * k, 16)]
         for i in (1, 2, 3):
             xx, zz = along(EARLY[k], i)
             send(
-                query.at[pl.ds(64 * group_of(axis, xx, y, zz, c) + 16 * k, 16)], block,
+                query.at[pl.ds(64 * group_of(axis, xx, y, zz, c) + 16 * k, 16)], met.at[4 - i],
                 s_q.at[k], r_q.at[k], at(xx, y, zz, c),
             )
-        pltpu.make_async_copy(
-            query.at[pl.ds(64 * group_of(axis, x, y, z, c) + 16 * k, 16)], block, r_q.at[k]
-        ).start()
+        for i in (1, 2, 3):
+            xx, zz = along(FIRST[k], i)
+            send(rows, met.at[0], s_v.at[k], r_v.at[k], at(xx, y, zz, c))
+        pltpu.make_async_copy(rows, met.at[0], r_q.at[k]).start()
         later(qbuf.at[k, 0, pl.ds(0, 3)], s_q.at[k])
 
     def pass_query(k):
@@ -179,20 +197,40 @@
         drain(met, r_q.at[k])
         for i in (1, 2, 3):
             xx, zz = along(FIRST[k], i)
-            send(met, met, s_v.at[k], r_v.at[k], at(xx, y, zz, c))
+            send(
+                met.at[pl.ds(1, 3)], met.at[pl.ds(1, 3)], s_v.at[k], r_v.at[k],
+                at(xx, y, zz, c),
+            )
         later(qbuf.at[k, pl.ds(0, 3)], s_v.at[k])
 
-    send_latents(1)
-    for k in range(4):
+    for k in (1, 0, 3, 2):
         send_query(k)
-    send_ropes(1)
-    for k in (0, 3, 2):
-        send_latents(k)
+    for core in range(2):
+        send_latents(FIRST_PAIR, core)
+    def half(j):
+        down = lax.broadcasted_iota(jnp.int32, (ROPE, 2 * ROPE), 0) + ROPE * j
+        right = lax.broadcasted_iota(jnp.int32, (ROPE, 2 * ROPE), 1)
+        return (down == right).astype(jnp.float32).astype(jnp.bfloat16)
+
+    halves = [half(0), half(1)]
+    loads[4].wait()
+    for n in range(4):
+        keys = raw[pl.ds(16 * n, 16)].reshape(8, 2, 64, ROPE)
+        both = sum(
+            jnp.dot(
+                keys[:, j].reshape(512, ROPE), halves[j], preferred_element_type=jnp.float32
+            )
+            for j in range(2)
+        )
+        rope[pl.ds(8 * n, 8)] = both.astype(jnp.bfloat16).reshape(8, 64, 2 * ROPE)
+    for k in (1, 0, 3, 2):
         send_ropes(k)
     loads[3].start()
 
     for k in (1, 0, 3, 2):
         pass_query(k)
+    for k in (0, 3):
+        send_latents(k, 0)
 
     def window(rows, n):
         left = 384 * (n % 2)
@@ -200,6 +238,8 @@
         return jnp.concatenate([block[:, left:left + 256], block[:, left + 256:left + 512]], axis=0)
 
     loads[0].wait()
+    for load in small:
+        load.wait()
     row = lax.broadcasted_iota(jnp.int32, (64, 64), 0)
     col = lax.broadcasted_iota(jnp.int32, (64, 64), 1)
     pick = (col == 8 * p + (row >> 3)).astype(jnp.float32).astype(jnp.bfloat16)
@@ -222,11 +262,8 @@
         zz = slot if axis == "z" else z
         return 64 * ((4 * xx + zz) * 8 + 2 * yy + core) + inner
 
-    def attend(k):
-        axis = PAIRS[k]
+    def queries_of(k):
         drain(qbuf.at[k, pl.ds(0, 3)], r_v.at[k])
-        spots = position(axis)
-        group = group_of(axis, x, y, z, c)
         both = qbuf[k].astype(jnp.float32).reshape(16, 2, 8, WIDTH)
         queries = []
         for j in range(2):
@@ -236,6 +273,13 @@
                 preferred_element_type=jnp.float32,
             )
             queries.append((rows[:, :KV_RANK].astype(jnp.bfloat16), turned.astype(jnp.bfloat16)))
+        return queries
+
+    def attend(k, queries=None):
+        queries = queries or queries_of(k)
+        axis = PAIRS[k]
+        spots = position(axis)
+        group = group_of(axis, x, y, z, c)
         drain(krope.at[k], r_o.at[k])
         drain(kbuf.at[k], r_k.at[k])
         sums, extras = [], []
@@ -276,7 +320,7 @@
                 pout.at[k, xx if FIRST[k] == "x" else zz], pmid.at[k, i - 1],
                 s_p.at[k], r_p.at[k], at(xx, y, zz, c),
             )
-        later(pmid.at[k], s_p.at[k])
+        once((0, k), lambda: drain(pmid.at[k], s_p.at[k]))
 
     def joined(blocks, own=None):
         extra = [block[..., KV_RANK:].astype(jnp.float32) for block in blocks]
@@ -308,13 +352,13 @@
             other = turn(here, i)
             xx, zz = (x, other) if first == "x" else (other, z)
             send(
-                pjoin.at[k, other], pin.at[k, place],
+                pjoin.at[k, i], pin.at[k, place],
                 s_j.at[k], r_j.at[k], at(xx, yy, zz, c),
             )
-        later(pin.at[k, pl.ds(0, 3)], s_j.at[k])
+        once((1, k), lambda: drain(pin.at[k, pl.ds(0, 3)], s_j.at[k]))
 
         def keep():
-            pltpu.make_async_copy(pjoin.at[k, here], pin.at[k, place], r_j.at[k]).start()
+            pltpu.make_async_copy(pjoin.at[k, 0], pin.at[k, place], r_j.at[k]).start()
 
         if axis == "y":
             keep()
@@ -324,14 +368,14 @@
             @pl.when(yy != y)
             def _():
                 send(
-                    pjoin.at[k, here], pin.at[k, place],
+                    pjoin.at[k, 0], pin.at[k, place],
                     s_j.at[k], r_j.at[k], at(x, yy, z, c),
                 )
 
             def left():
                 pl.when(yy != y)(lambda: drain(pin.at[k, 0], s_j.at[k]))
 
-            pending.append(left)
+            once((2, k), left)
 
     def join_last(k):
         drain(pin.at[k], r_j.at[k])
@@ -347,17 +391,36 @@
         for b in range(KV_RANK // 128):
             lat[b, pl.ds(16 * k, 16), :] = summed[:, 128 * b:128 * b + 128]
 
-    attend(1)
-    attend(0)
-    join_first(1)
-    attend(3)
-    join_first(0)
-    attend(2)
-    join_first(3)
-    for k in (1, 0):
-        join_last(k)
-    join_first(2)
-    for k in (3, 2):
+    queries = queries_of(FIRST_PAIR)
+    send_latents(LAST, 0)
+    for core in range(2):
+        latents_left(FIRST_PAIR, core)
+    send_latents(LAST, 1)
+    attend(FIRST_PAIR, queries)
+    for k in (0, 3):
+        latents_left(k, 0)
+        send_latents(k, 1)
+
+    @pl.when(c == 0)
+    def _():
+        attend(0)
+        attend(3)
+        join_first(1)
+        attend(2)
+
+    @pl.when(c == 1)
+    def _():
+        join_first(1)
+        attend(0)
+        attend(3)
+        attend(2)
+
+    for k in (0, 3, 2):
+        join_first(k)
+    latents_left(LAST, 0)
+    for k in (0, 3, 2):
+        latents_left(k, 1)
+    for k in (1, 0, 3, 2):
         join_last(k)
 
     loads[1].wait()
@@ -486,6 +549,11 @@
         logits = logits + lb[n].astype(jnp.float32)
     low, high = logits[:8] * norm, logits[8:] * norm
 
+    raws[:, pl.ds(0, HALF)] = low
+    raws[:, pl.ds(HALF, vocab - HALF)] = high[:, : vocab - HALF]
+    write = pltpu.make_async_copy(raws, out, l_w.at[0])
+    write.start()
+
     column = lax.broadcasted_iota(jnp.int32, (8, HALF), 1)
     high = jnp.where(column < vocab - HALF, high, FILL)
     slot_rows = lax.broadcasted_iota(jnp.int32, (8, 64), 0) + 8 * p
@@ -515,14 +583,17 @@
     )
     picked = picked + jnp.sum(others[:, :, 2:3], axis=0)
     normalizer = best + jnp.log(total)
-    out[:, pl.ds(0, HALF)] = low - normalizer
-    out[:, pl.ds(HALF, vocab - HALF)] = (high - normalizer)[:, : vocab - HALF]
+    tail[...] = jnp.where(lane8 == 0, normalizer, picked - normalizer)
+    write.wait()
+    finish()
+
+
+def finish_kernel(logits, tail, out, tgt):
+    out[...] = logits[...] - tail[:, 0:1]
     square = lax.broadcasted_iota(jnp.int32, (8, 8), 0) == lax.broadcasted_iota(
         jnp.int32, (8, 8), 1
     )
-    tgt[...] = jnp.sum(jnp.where(square, picked - normalizer, 0.0), axis=0, keepdims=True)
-
-    finish()
+    tgt[...] = jnp.sum(jnp.where(square, tail[:, 1:2], 0.0), axis=0, keepdims=True)
 
 
 def body(
@@ -533,18 +604,23 @@
     bf16, f32 = jnp.bfloat16, jnp.float32
     vmem = pl.BlockSpec(memory_space=pltpu.VMEM)
     anywhere = pl.BlockSpec(memory_space=pl.ANY)
-    smem = pl.BlockSpec(memory_space=pltpu.SMEM)
     dma = pltpu.SemaphoreType.DMA
-    logprobs, target = pl.pallas_call(
+    logits, tail = pl.pallas_call(
         kernel,
         out_shape=(
             jax.ShapeDtypeStruct((8, vocab), f32),
-            jax.ShapeDtypeStruct((1, 8), f32),
+            jax.ShapeDtypeStruct((8, 128), f32),
         ),
-        in_specs=[smem, anywhere, anywhere, vmem, vmem, vmem, vmem, vmem,
-                  anywhere, anywhere, anywhere],
-        out_specs=(vmem, vmem),
+        in_specs=[anywhere] * 11,
+        out_specs=(anywhere, vmem),
         scratch_shapes=[
+            pltpu.SMEM((64,), jnp.int32),
+            pltpu.VMEM((64, WIDTH), bf16),
+            pltpu.VMEM((1, 64), jnp.int32),
+            pltpu.VMEM((1, 64), jnp.int32),
+            pltpu.VMEM((64, columns), bf16),
+            pltpu.VMEM((columns,), bf16),
+            pltpu.VMEM((8, vocab), f32),
             pltpu.VMEM((4, 2, 512, KV_RANK), bf16),
             pltpu.VMEM((64, 64, ROPE), bf16),
             pltpu.VMEM((32, 64, 2 * ROPE), bf16),
@@ -571,8 +647,9 @@
             pltpu.VMEM((3, 16, HALF), bf16),
             pltpu.VMEM((8, 128), f32),
             pltpu.VMEM((15, 8, 128), f32),
-            dma((4,)), dma((4,)), dma((4,)), dma((4,)), dma((4,)), dma((4,)), dma((4,)), dma((4,)), dma((4,)), dma((4,)), dma((4,)), dma((4,)),
-            dma((5,)),
+            dma((8,)), dma((4,)), dma((4,)), dma((4,)), dma((4,)), dma((4,)), dma((4,)), dma((4,)),
+            dma((4,)), dma((4,)), dma((4,)), dma((4,)),
+            dma((11,)),
             dma((7,)), dma((7,)), dma((1,)), dma((1,)), dma((15,)), dma((15,)),
             dma((1,)), dma((1,)), dma((CHUNKS,)), dma((CHUNKS,)), dma((CHUNKS,)),
             dma((CHUNKS,)), dma((1,)), dma((1,)),
@@ -594,6 +671,14 @@
         out_weight,
         lm_weight.T,
     )
+    logprobs, target = pl.pallas_call(
+        finish_kernel,
+        out_shape=(
+            jax.ShapeDtypeStruct((8, vocab), f32),
+            jax.ShapeDtypeStruct((1, 8), f32),
+        ),
+        name="log_probabilities",
+    )(logits, tail)
     return logprobs, target.reshape(8)
 
 

time: 88.2 us -> 86.5 us (0.981)
  local copies, waits for them, and re-layouts: 2.8 us -> 0 us
  Pallas kernels: 84.5 us -> 85.7 us
    unnamed x2 -> x0, local copies, waits for them, and re-layouts: 2.8 us -> none
    pallas_call x0 -> x1, Pallas kernels: none -> 1.75 us  [body(): pl.pallas_call(finish_kernel, out_shape=(jax.ShapeDtypeStruct((8, vocab),...]
where the time goes in v4:
time: 86.5 us; the launch traced here: 86.4 us
  Pallas kernels  85.7 us (99%)
    pallas_call x1, Pallas kernels, body(): pl.pallas_call(kernel, out_shape=(jax.ShapeDtypeStruct((8, vocab), f32),...  84 us
    pallas_call x1, Pallas kernels, body(): pl.pallas_call(finish_kernel, out_shape=(jax.ShapeDtypeStruct((8, vocab),...  1.75 us

profile of v4, /device:TPU:0, one launch (start us, length us, event | category | flops | bytes accessed | tf_op | source)
XLA Modules:
  0.0 86.4 jit_solution(9988487787318589307)
XLA Ops:
  0.6 84.0 %decode_step.1 = (f32[8,8080]{1,0:T(8,128)}, f32[8,128]{1,0:T(8,128)}) custom-call(s32[64]{0:T(128)} %lens_in.1, bf16[64,64,576]{2,1,0:T(8,128)(2,1)} %cache.1, bf16[512,576]{1,0:T(8,128)(2,1)} %bitcast.6, bf16[64,576]{1,0:T(8,128)(2,1)} %newl_in.1, s32[1,64]{1,0:T(1,128)} %bitcast.7, s32[1,64]{1,0:T(1,128)} %bitcast.8, bf16[64,896]{1,0:T(8,128)(2,1)} %resid_in.1, ...), custom_call_target="tpu_custom_call" | custom-call | tf_op jit(solution)/shard_map/decode_step/pallas_call | solution.py:608
  84.6 1.7 %log_probabilities.1 = (f32[8,8080]{1,0:T(8,128)}, f32[1,8]{1,0:T(1,128)}) custom-call(f32[8,8080]{1,0:T(8,128)} %get-tuple-element.6.logits, f32[8,128]{1,0:T(8,128)} %get-tuple-element.7.tail), custom_call_target="tpu_custom_call" | custom-call | tf_op jit(solution)/shard_map/log_probabilities/pallas_call | solution.py:674

commit v5 on v4

--- a/solution.py
+++ b/solution.py
@@ -72,8 +72,11 @@
     def signal(device):
         pl.semaphore_signal(barrier, inc=1, device_id=device, device_id_type=MESH)
 
+    hops = (0, 1, 2, 1)
     DEC = [(i, j) for i in range(4) for j in range(4) if (i, j) != (0, 0)]
+    DEC.sort(key=lambda ij: -hops[ij[0]] - hops[ij[1]])
     PRE = [(i, j) for i in range(4) for j in range(2) if (i, j) != (0, 0)]
+    PRE.sort(key=lambda ij: -hops[ij[0]] - ij[1])
 
     loads = [
         pltpu.make_async_copy(query.at[pl.ds(64 * p, 64)], qown, l_w.at[0]),
@@ -87,10 +90,10 @@
         signal(at(turn(x, i), y, turn(z, j), c))
     for i, j in PRE:
         signal(at(x, turn(y, i), z, lax.rem(c + j, 2)))
-    for i in (1, 2, 3):
+    for i in (2, 1, 3):
         signal(at(turn(x, i), y, z, 1 - c))
         signal(at(x, y, turn(z, i), 1 - c))
-    for i in (1, 2, 3):
+    for i in (2, 1, 3):
         signal(at(y, turn(y, i), z, c))
         signal(at(x, turn(y, i), y, c))
 
@@ -146,7 +149,7 @@
             first = 8 * group_of(axis, xx, yy, zz, cc) + 2 * k
             return cache.at[pl.ds(first, 2), :, pl.ds(0, KV_RANK)]
 
-        for i in (1, 2, 3):
+        for i in (2, 1, 3):
             xx = turn(x, i) if axis == "x" else x
             yy = turn(y, i) if axis == "y" else y
             zz = turn(z, i) if axis == "z" else z
@@ -180,13 +183,13 @@
         axis = PAIRS[k]
         met = qbuf.at[k, coordinate(FIRST[k])]
         rows = query.at[pl.ds(64 * group_of(axis, x, y, z, c) + 16 * k, 16)]
-        for i in (1, 2, 3):
+        for i in (2, 1, 3):
             xx, zz = along(EARLY[k], i)
             send(
                 query.at[pl.ds(64 * group_of(axis, xx, y, zz, c) + 16 * k, 16)], met.at[4 - i],
                 s_q.at[k], r_q.at[k], at(xx, y, zz, c),
             )
-        for i in (1, 2, 3):
+        for i in (2, 1, 3):
             xx, zz = along(FIRST[k], i)
             send(rows, met.at[0], s_v.at[k], r_v.at[k], at(xx, y, zz, c))
         pltpu.make_async_copy(rows, met.at[0], r_q.at[k]).start()
@@ -195,7 +198,7 @@
     def pass_query(k):
         met = qbuf.at[k, coordinate(FIRST[k])]
         drain(met, r_q.at[k])
-        for i in (1, 2, 3):
+        for i in (2, 1, 3):
             xx, zz = along(FIRST[k], i)
             send(
                 met.at[pl.ds(1, 3)], met.at[pl.ds(1, 3)], s_v.at[k], r_v.at[k],
@@ -314,7 +317,7 @@
         for n in range(4):
             pout[k, n, :, :, pl.ds(0, KV_RANK)] = sums[n]
             pout[k, n, :, :, pl.ds(KV_RANK, EXTRA)] = extras[n]
-        for i in (1, 2, 3):
+        for i in (2, 1, 3):
             xx, zz = along(FIRST[k], i)
             send(
                 pout.at[k, xx if FIRST[k] == "x" else zz], pmid.at[k, i - 1],
@@ -348,7 +351,7 @@
         yy = {"x": x, "y": y, "z": z}[axis]
         place = y if axis != "y" else (z if first == "x" else x)
         here = z if first == "x" else x
-        for i in (1, 2, 3):
+        for i in (2, 1, 3):
             other = turn(here, i)
             xx, zz = (x, other) if first == "x" else (other, z)
             send(
@@ -508,7 +511,7 @@
         ls[c, :, :, lanes] = (
             ls[c, :, :, lanes].astype(jnp.float32) + lr[:, :, lanes].astype(jnp.float32)
         ).astype(jnp.bfloat16)
-        for step in (1, 2, 3):
+        for step in (2, 1, 3):
             yy = turn(y, step)
             send(
                 ls.at[c, yy, :, lanes], lb.at[step - 1, :, lanes],

time: 86.5 us -> 82.5 us (0.954)
  Pallas kernels: 85.7 us -> 81.7 us
    pallas_call x1, Pallas kernels: 84 us -> 79.9 us  [body(): pl.pallas_call(kernel, out_shape=(jax.ShapeDtypeStruct((8, vocab), f32),...]
where the time goes in v5:
time: 82.5 us; the launch traced here: 82.3 us
  Pallas kernels  81.7 us (99%)
    pallas_call x1, Pallas kernels, body(): pl.pallas_call(kernel, out_shape=(jax.ShapeDtypeStruct((8, vocab), f32),...  79.9 us
    pallas_call x1, Pallas kernels, body(): pl.pallas_call(finish_kernel, out_shape=(jax.ShapeDtypeStruct((8, vocab),...  1.75 us

profile of v5, /device:TPU:0, one launch (start us, length us, event | category | flops | bytes accessed | tf_op | source)
XLA Modules:
  0.0 82.3 jit_solution(11545489227425255828)
XLA Ops:
  0.6 79.9 %decode_step.1 = (f32[8,8080]{1,0:T(8,128)}, f32[8,128]{1,0:T(8,128)}) custom-call(s32[64]{0:T(128)} %lens_in.1, bf16[64,64,576]{2,1,0:T(8,128)(2,1)} %cache.1, bf16[512,576]{1,0:T(8,128)(2,1)} %bitcast.6, bf16[64,576]{1,0:T(8,128)(2,1)} %newl_in.1, s32[1,64]{1,0:T(1,128)} %bitcast.7, s32[1,64]{1,0:T(1,128)} %bitcast.8, bf16[64,896]{1,0:T(8,128)(2,1)} %resid_in.1, ...), custom_call_target="tpu_custom_call" | custom-call | tf_op jit(solution)/shard_map/decode_step/pallas_call | solution.py:611
  80.6 1.7 %log_probabilities.1 = (f32[8,8080]{1,0:T(8,128)}, f32[1,8]{1,0:T(1,128)}) custom-call(f32[8,8080]{1,0:T(8,128)} %get-tuple-element.6.logits, f32[8,128]{1,0:T(8,128)} %get-tuple-element.7.tail), custom_call_target="tpu_custom_call" | custom-call | tf_op jit(solution)/shard_map/log_probabilities/pallas_call | solution.py:677

commit v6 on v5

--- a/solution.py
+++ b/solution.py
@@ -86,6 +86,18 @@
         pltpu.make_async_copy(cache.at[:, :, pl.ds(KV_RANK, ROPE)], raw, l_w.at[4]),
     ]
     barrier = pltpu.get_barrier_semaphore()
+    for i in (2, 1, 3):
+        signal(at(y, turn(y, i), z, c))
+        signal(at(x, turn(y, i), y, c))
+
+    @pl.when(x != y)
+    def _():
+        signal(at(y, y, z, c))
+
+    @pl.when(z != y)
+    def _():
+        signal(at(x, y, y, c))
+
     for i, j in DEC:
         signal(at(turn(x, i), y, turn(z, j), c))
     for i, j in PRE:
@@ -93,18 +105,6 @@
     for i in (2, 1, 3):
         signal(at(turn(x, i), y, z, 1 - c))
         signal(at(x, y, turn(z, i), 1 - c))
-    for i in (2, 1, 3):
-        signal(at(y, turn(y, i), z, c))
-        signal(at(x, turn(y, i), y, c))
-
-    @pl.when(x != y)
-    def _():
-        signal(at(y, y, z, c))
-
-    @pl.when(z != y)
-    def _():
-        signal(at(x, y, y, c))
-
     small = [
         pltpu.make_async_copy(src, dst, l_w.at[5 + n])
         for n, (src, dst) in enumerate([
@@ -437,12 +437,11 @@
         [jnp.concatenate(values[:4], axis=1), jnp.concatenate(values[4:], axis=1)], axis=0
     )
     hv[p] = packed.astype(jnp.bfloat16)
-    for n, (i, j) in enumerate(PRE):
-        send(hv.at[p], hv.at[p], s_h.at[n], r_h.at[n], at(x, turn(y, i), z, lax.rem(c + j, 2)))
-        later(hv.at[0], s_h.at[n])
+    for i, j in PRE:
+        send(hv.at[p], hv.at[p], s_h.at[0], r_h.at[0], at(x, turn(y, i), z, lax.rem(c + j, 2)))
+    later(hv.at[pl.ds(0, 7)], s_h.at[0])
     loads[2].wait()
-    for n in range(7):
-        drain(hv.at[0], r_h.at[n])
+    drain(hv.at[pl.ds(0, 7)], r_h.at[0])
 
     heads = hv[...].astype(jnp.float32).reshape(8, 2, 8, KV_RANK)
     part = jnp.zeros((64, owv.shape[1]), jnp.float32)
@@ -479,11 +478,10 @@
     agb[d, :, pl.ds(256, 128)] = jnp.where(
         lane16 == 0, first, jnp.where(lane16 == 1, second, third)
     ).astype(jnp.bfloat16)
-    for n, (i, j) in enumerate(DEC):
-        send(agb.at[d], agb.at[d], s_a.at[n], r_a.at[n], at(turn(x, i), y, turn(z, j), c))
-        later(agb.at[0], s_a.at[n])
-    for n in range(15):
-        drain(agb.at[0], r_a.at[n])
+    for i, j in DEC:
+        send(agb.at[d], agb.at[d], s_a.at[0], r_a.at[0], at(turn(x, i), y, turn(z, j), c))
+    later(agb.at[pl.ds(0, 15)], s_a.at[0])
+    drain(agb.at[pl.ds(0, 15)], r_a.at[0])
     gathered = agb[...].astype(jnp.float32).reshape(8, 2, 2, 8, 384)
     squares = sum(
         gathered[:, h, 0, :, 256 + n:257 + n] for h in range(2) for n in range(3)
@@ -577,7 +575,7 @@
     sms[...] = mine
     for n, (i, j) in enumerate(DEC):
         send(sms, smr.at[n], s_m.at[0], r_m.at[0], at(turn(x, i), y, turn(z, j), c))
-    later(smr, s_m.at[0])
+    finish()
     drain(smr, r_m.at[0])
     others = smr[...]
     best = jnp.maximum(jnp.max(others[:, :, 0:1], axis=0), top)
@@ -588,7 +586,7 @@
     normalizer = best + jnp.log(total)
     tail[...] = jnp.where(lane8 == 0, normalizer, picked - normalizer)
     write.wait()
-    finish()
+    drain(smr, s_m.at[0])
 
 
 def finish_kernel(logits, tail, out, tgt):
@@ -653,7 +651,7 @@
             dma((8,)), dma((4,)), dma((4,)), dma((4,)), dma((4,)), dma((4,)), dma((4,)), dma((4,)),
             dma((4,)), dma((4,)), dma((4,)), dma((4,)),
             dma((11,)),
-            dma((7,)), dma((7,)), dma((1,)), dma((1,)), dma((15,)), dma((15,)),
+            dma((1,)), dma((1,)), dma((1,)), dma((1,)), dma((1,)), dma((1,)),
             dma((1,)), dma((1,)), dma((CHUNKS,)), dma((CHUNKS,)), dma((CHUNKS,)),
             dma((CHUNKS,)), dma((1,)), dma((1,)),
         ],

time: 82.5 us -> 82 us (level)
  no operation moved by 1% of the time
where the time goes in v6:
time: 82 us; the launch traced here: 81.9 us
  Pallas kernels  81.2 us (99%)
    pallas_call x1, Pallas kernels, body(): pl.pallas_call(kernel, out_shape=(jax.ShapeDtypeStruct((8, vocab), f32),...  79.5 us
    pallas_call x1, Pallas kernels, body(): pl.pallas_call(finish_kernel, out_shape=(jax.ShapeDtypeStruct((8, vocab),...  1.75 us

profile of v6, /device:TPU:0, one launch (start us, length us, event | category | flops | bytes accessed | tf_op | source)
XLA Modules:
  0.0 81.9 jit_solution(12041487372448856768)
XLA Ops:
  0.6 79.5 %decode_step.1 = (f32[8,8080]{1,0:T(8,128)}, f32[8,128]{1,0:T(8,128)}) custom-call(s32[64]{0:T(128)} %lens_in.1, bf16[64,64,576]{2,1,0:T(8,128)(2,1)} %cache.1, bf16[512,576]{1,0:T(8,128)(2,1)} %bitcast.6, bf16[64,576]{1,0:T(8,128)(2,1)} %newl_in.1, s32[1,64]{1,0:T(1,128)} %bitcast.7, s32[1,64]{1,0:T(1,128)} %bitcast.8, bf16[64,896]{1,0:T(8,128)(2,1)} %resid_in.1, ...), custom_call_target="tpu_custom_call" | custom-call | tf_op jit(solution)/shard_map/decode_step/pallas_call | solution.py:609
  80.1 1.7 %log_probabilities.1 = (f32[8,8080]{1,0:T(8,128)}, f32[1,8]{1,0:T(1,128)}) custom-call(f32[8,8080]{1,0:T(8,128)} %get-tuple-element.6.logits, f32[8,128]{1,0:T(8,128)} %get-tuple-element.7.tail), custom_call_target="tpu_custom_call" | custom-call | tf_op jit(solution)/shard_map/log_probabilities/pallas_call | solution.py:675

commit v7 on v6

--- a/solution.py
+++ b/solution.py
@@ -487,10 +487,6 @@
         gathered[:, h, 0, :, 256 + n:257 + n] for h in range(2) for n in range(3)
     )
     sqs[...] = jnp.broadcast_to(squares, (8, 8, 128))
-    for n, (i, j) in enumerate(PRE):
-        yy, cc = turn(y, i), lax.rem(c + j, 2)
-        send(sqs.at[2 * yy + cc], sqr.at[n], s_s.at[0], r_s.at[0], at(x, yy, z, cc))
-    later(sqr, s_s.at[0])
     scaled = jnp.concatenate(
         [
             gathered[:, 0, 0, :, 0:256].reshape(64, 256),
@@ -534,7 +530,12 @@
             s_c.at[i], r_c.at[i], at(x, y, z, 1 - c),
         )
         later(lr.at[:, :, lanes], s_c.at[i])
-        if i > 0:
+        if i == 0:
+            for n, (up, over) in enumerate(PRE):
+                yy, cc = turn(y, up), lax.rem(c + over, 2)
+                send(sqs.at[2 * yy + cc], sqr.at[n], s_s.at[0], r_s.at[0], at(x, yy, z, cc))
+            later(sqr, s_s.at[0])
+        else:
             join_cores(i - 1)
     join_cores(CHUNKS - 1)
 
@@ -550,11 +551,6 @@
         logits = logits + lb[n].astype(jnp.float32)
     low, high = logits[:8] * norm, logits[8:] * norm
 
-    raws[:, pl.ds(0, HALF)] = low
-    raws[:, pl.ds(HALF, vocab - HALF)] = high[:, : vocab - HALF]
-    write = pltpu.make_async_copy(raws, out, l_w.at[0])
-    write.start()
-
     column = lax.broadcasted_iota(jnp.int32, (8, HALF), 1)
     high = jnp.where(column < vocab - HALF, high, FILL)
     slot_rows = lax.broadcasted_iota(jnp.int32, (8, 64), 0) + 8 * p
@@ -575,6 +571,10 @@
     sms[...] = mine
     for n, (i, j) in enumerate(DEC):
         send(sms, smr.at[n], s_m.at[0], r_m.at[0], at(turn(x, i), y, turn(z, j), c))
+    raws[:, pl.ds(0, HALF)] = low
+    raws[:, pl.ds(HALF, vocab - HALF)] = high[:, : vocab - HALF]
+    write = pltpu.make_async_copy(raws, out, l_w.at[0])
+    write.start()
     finish()
     drain(smr, r_m.at[0])
     others = smr[...]

time: 82 us -> 82 us (level)
  no operation moved by 1% of the time
where the time goes in v7:
time: 82 us; the launch traced here: 81.9 us
  Pallas kernels  81.2 us (99%)
    pallas_call x1, Pallas kernels, body(): pl.pallas_call(kernel, out_shape=(jax.ShapeDtypeStruct((8, vocab), f32),...  79.5 us
    pallas_call x1, Pallas kernels, body(): pl.pallas_call(finish_kernel, out_shape=(jax.ShapeDtypeStruct((8, vocab),...  1.75 us

profile of v7, /device:TPU:0, one launch (start us, length us, event | category | flops | bytes accessed | tf_op | source)
XLA Modules:
  0.0 81.9 jit_solution(17316590316809140961)
XLA Ops:
  0.6 79.5 %decode_step.1 = (f32[8,8080]{1,0:T(8,128)}, f32[8,128]{1,0:T(8,128)}) custom-call(s32[64]{0:T(128)} %lens_in.1, bf16[64,64,576]{2,1,0:T(8,128)(2,1)} %cache.1, bf16[512,576]{1,0:T(8,128)(2,1)} %bitcast.6, bf16[64,576]{1,0:T(8,128)(2,1)} %newl_in.1, s32[1,64]{1,0:T(1,128)} %bitcast.7, s32[1,64]{1,0:T(1,128)} %bitcast.8, bf16[64,896]{1,0:T(8,128)(2,1)} %resid_in.1, ...), custom_call_target="tpu_custom_call" | custom-call | tf_op jit(solution)/shard_map/decode_step/pallas_call | solution.py:609
  80.1 1.7 %log_probabilities.1 = (f32[8,8080]{1,0:T(8,128)}, f32[1,8]{1,0:T(1,128)}) custom-call(f32[8,8080]{1,0:T(8,128)} %get-tuple-element.6.logits, f32[8,128]{1,0:T(8,128)} %get-tuple-element.7.tail), custom_call_target="tpu_custom_call" | custom-call | tf_op jit(solution)/shard_map/log_probabilities/pallas_call | solution.py:675
